TPU v7x, 256 devices: a whole 4x4x8 slice. The times are simulated.
256 devices in a mesh: station: 64 (over x, z_lo, y, core), window: 4 (over z_hi).
Axes of the slice: x: 4, y: 4, z: 8 (z_hi: 4, z_lo: 2; z = z_hi * 2 + z_lo), core: 2. Of those that a mesh axis runs over, the one named last changes fastest.
Arguments:
- spectra: bfloat16 [256, 24, 3, 2, 4608], P('station', 'window'), may hold values from -6 to 6
- valid_mask: int32 [256, 24], P('station', 'window'), may hold values 0 or 1
- plan: int32 [2], replicated, may hold values from 0 to 63
Outputs:
- stacks: float32 [4, 2, 3, 256, 3, 512], P('window', None, None, 'station')
Inputs may be any that keep to these rules, and one draw needn't show every extreme that they name: `plan`: each entry is a station block index.
All inputs are finite; a program needn't handle non-finite values. No bound on the sum of `valid_mask` on one device may be relied on, other than what follows from the above.
Results may differ from a plain program's by a relative error of at most 0.0003.
Values may be sent and summed in bfloat16 or wider, within the bound.
No kernel may reach another device: no remote copies, remote signals or barrier semaphores. Data moves between devices by JAX's collectives and lax.ppermute only.
A program may use at most 128 MiB of HBM per device.

v0:
```python
import math

import jax
import jax.numpy as jnp
from jax import lax
from jax.sharding import PartitionSpec as P

LAGS = 512
NW = 18000
STEPS = 2


def broadcast(block, axis, owner):
    block = jnp.where(lax.axis_index(axis) == owner, block, jnp.zeros_like(block))
    return lax.psum(block, axis)


def make_basis(bins, lag_count, samples, hours):
    freqs = jnp.arange(bins, dtype=jnp.int32)[:, None]
    shifts = jnp.arange(lag_count, dtype=jnp.int32)[None, :] - lag_count // 2
    phases = jnp.mod(freqs * shifts, samples)
    angles = phases.astype(jnp.float32) * (2.0 * math.pi / samples)
    factor = 1.0 / math.sqrt(2.0 * bins * hours)
    return jnp.concatenate([jnp.cos(angles), -jnp.sin(angles)], 0) * factor


def cross_local(left, right):
    left_count = left.shape[0]
    right_count = right.shape[0]
    bins = left.shape[-1]
    empty = jnp.zeros((left_count, 3, right_count, 3, bins), jnp.float32)

    def add_hour(hour, totals):
        left_hour = lax.dynamic_index_in_dim(left, hour, 1, keepdims=False).astype(jnp.float32)
        right_hour = lax.dynamic_index_in_dim(right, hour, 1, keepdims=False).astype(jnp.float32)
        left_re = left_hour[:, :, 0][:, :, None, None, :]
        left_im = left_hour[:, :, 1][:, :, None, None, :]
        right_re = right_hour[:, :, 0][None, None, :, :, :]
        right_im = right_hour[:, :, 1][None, None, :, :, :]
        real_part = totals[0] + (left_re * right_re + left_im * right_im)
        imag_part = totals[1] + (left_re * right_im - left_im * right_re)
        return (real_part, imag_part)

    return lax.fori_loop(0, left.shape[1], add_hour, (empty, empty))


def inverse_lags(real_part, imag_part, lag_basis):
    joined = jnp.concatenate([real_part, imag_part], -1)
    shape = joined.shape
    result = jnp.dot(
        joined.reshape(-1, shape[-1]),
        lag_basis,
        precision=lax.Precision.HIGHEST,
        preferred_element_type=jnp.float32,
    )
    return result.reshape(shape[:-1] + (lag_basis.shape[1],))


def body(spectra, valid_mask, plan):
    windows = lax.axis_size("window")
    hours = spectra.shape[1] * windows
    keep_rows = spectra.shape[0] // windows
    masked = spectra * valid_mask.astype(jnp.bfloat16)[:, :, None, None, None]
    lag_basis = make_basis(spectra.shape[4], LAGS, NW, hours)
    results = []
    for which_step in range(STEPS):
        owner_rows = broadcast(masked, "station", plan[which_step])
        real_part, imag_part = cross_local(owner_rows, masked)

        def lag_term(offset, amount, real_part=real_part, imag_part=imag_part):
            return inverse_lags(real_part, imag_part, lag_basis)

        stacked = lax.psum_scatter(
            lag_term(jnp.int32(0), lax.axis_size("window") * keep_rows),
            "window",
            scatter_dimension=0,
            tiled=True,
        )
        results.append(stacked)
    return jnp.stack(results, 1)


def solution(mesh):
    return jax.shard_map(
        body,
        mesh=mesh,
        in_specs=(P("station", "window", None, None, None), P("station", "window"), P()),
        out_specs=P("window", None, None, "station", None, None),
        check_vma=False,
    )
```

profile of v0, /device:TPU:1, one launch (start us, length us, event | category | flops | bytes accessed | tf_op | source)
XLA Modules:
  0.0 804.7 jit_solution(2443834149297879239)
XLA Ops:
  7.3 1.3 fusion.23
  9.9 5.0 copy_multiply_fusion
  15.0 40.2 %fusion.11 = (f32[4608,512]{1,0:T(8,128)}, f32[4608,512]{1,0:T(8,128)}) fusion(s32[512]{0:T(512)S(1)} %iota_add_fusion), kind=kLoop, calls=%fused_computation.29 | loop fusion | flops 23592960 | bytes 18876416 | tf_op jit(solution)/shard_map/cos | solution.py:24
  55.2 520.0 %all-reduce.9.cloned.1.call-done = (bf16[4,6,3,2,4608]{4,2,0,3,1:T(4,128)(2,1)}, bf16[4,6,3,2,4608]{4,2,0,3,1:T(4,128)(2,1)}) async-done(((bf16[4,6,3,2,4608]{4,2,0,3,1:T(4,128)(2,1)}, bf16[4,6,3,2,4608]{4,2,0,3,1:T(4,128)(2,1)}), (bf16[4,6,3,2,4608]{4,2,0,3,1:T(4,128)(2,1)}, bf16[4,6,3,2,4608]{4,2,0,3,1:T(4,128)(2,1)})) %all-reduce.9.cloned.1.call-update) | async-done | bytes 2654224 | tf_op jit(solution)/shard_map/psum | solution.py:15
  575.3 54.6 %while.33 = (s32[]{:T(128)}, f32[4,3,4,3,4608]{4,3,2,1,0:T(4,128)}, f32[4,3,4,3,4608]{4,3,2,1,0:T(4,128)}, bf16[4,6,3,2,4608]{4,2,0,3,1:T(4,128)(2,1)}, bf16[4,6...) while((s32[]{:T(128)}, f32[4,3,4,3,4608]{4,3,2,1,0:T(4,128)}, ...), condition=%wide.region_6.7_spmd.clone, body=%wide.region_5.6_spmd.clone.sunk | while | flops 6856707 | bytes 35831960 | solution.py:44
  575.3 1.3 bitcast_convert_fusion.7
  577.4 3.9 select_add_fusion.7
  581.4 1.7 copy-done.4
  583.1 1.3 bitcast_convert_fusion.7
  585.3 5.4 select_add_fusion.7
  590.7 1.7 copy-done.4
  592.5 1.3 bitcast_convert_fusion.7
  594.7 5.4 select_add_fusion.7
  600.1 1.7 copy-done.4
  601.8 1.3 bitcast_convert_fusion.7
  604.0 5.4 select_add_fusion.7
  609.4 1.7 copy-done.4
  611.2 1.3 bitcast_convert_fusion.7
  613.4 5.4 select_add_fusion.7
  618.8 1.7 copy-done.4
  620.5 1.3 bitcast_convert_fusion.7
  622.7 5.4 select_add_fusion.7
  628.1 1.7 copy-done.4
  629.9 4.5 copy.15
  634.3 40.9 %while.32 = (s32[]{:T(128)}, f32[4,3,4,3,4608]{4,3,2,1,0:T(4,128)}, f32[4,3,4,3,4608]{4,3,2,1,0:T(4,128)S(1)}, bf16[4,6,3,2,4608]{4,2,0,3,1:T(4,128)(2,1)}, bf16...) while((s32[]{:T(128)}, f32[4,3,4,3,4608]{4,3,2,1,0:T(4,128)}, ...), condition=%wide.region_2.3_spmd.clone, body=%wide.region_1.2_spmd.clone.sunk | while | flops 6856707 | bytes 35831960 | solution.py:44
  634.3 1.3 bitcast_convert_fusion.6
  636.5 2.8 select_add_fusion.6
  639.3 1.8 copy-done.1
  641.2 1.3 bitcast_convert_fusion.6
  643.3 2.8 select_add_fusion.6
  646.1 1.8 copy-done.1
  648.0 1.3 bitcast_convert_fusion.6
  650.1 2.8 select_add_fusion.6
  653.0 1.8 copy-done.1
  654.8 1.3 bitcast_convert_fusion.6
  657.0 2.8 select_add_fusion.6
  659.8 1.8 copy-done.1
  663.8 2.8 select_add_fusion.6
  666.6 1.8 copy-done.1
  670.6 2.8 select_add_fusion.6
  673.4 1.8 copy-done.1
  675.2 2.5 copy.13
  677.7 2.5 copy.12
  680.3 2.6 copy.14
  682.8 27.6 %fusion.1 = f32[4,3,4,3,512]{4,2,3,1,0:T(4,128)} fusion(f32[4608,512]{1,0:T(8,128)} %get-tuple-element.279, f32[4608,512]{1,0:T(8,128)} %get-tuple-element.278, f32[4,3,4,3,4608]{4,2,3,1,0:T(4,128)S(1)} %copy-done.6, f32[4,3,4,3,4608]{4,2,3,1,0:T(4,128)} %copy.14), kind=kOutput, calls=%fused_computation.18 | convolution fusion | flops 8164491264 | bytes 24477696 | tf_op jit(solution)/shard_map/dot_general | solution.py:50
  710.4 28.6 %fusion.3 = f32[4,3,4,3,512]{4,2,3,1,0:T(4,128)} fusion(f32[4608,512]{1,0:T(8,128)} %get-tuple-element.279, f32[4608,512]{1,0:T(8,128)} %get-tuple-element.278, f32[4,3,4,3,4608]{4,2,3,1,0:T(4,128)} %copy.13, f32[4,3,4,3,4608]{4,2,3,1,0:T(4,128)} %copy.12), kind=kOutput, calls=%fused_computation.19 | convolution fusion | flops 8164491264 | bytes 24477696 | tf_op jit(solution)/shard_map/dot_general | solution.py:50
  739.7 55.9 %all-reduce.7.cloned.1.call-done = (f32[4,3,4,3,512]{4,2,3,1,0:T(4,128)}, f32[4,3,4,3,512]{4,2,3,1,0:T(4,128)}) async-done(((f32[4,3,4,3,512]{4,2,3,1,0:T(4,128)}, f32[4,3,4,3,512]{4,2,3,1,0:T(4,128)}), (f32[4,3,4,3,512]{4,2,3,1,0:T(4,128)}, f32[4,3,4,3,512]{4,2,3,1,0:T(4,128)})) %all-reduce.7.cloned.1.call-update) | async-done | bytes 589840
  795.6 1.6 dynamic-slice_bitcast_fusion
  (83 shorter events, 15.1 us)
Async XLA Ops:
  6.5 568.7 %all-reduce.9.cloned.1.call-start = ((), (), s32[]{:S(2)}) async-start(), calls=%async_computation.1 | async-start | bytes 7077888 | tf_op jit(solution)/shard_map/psum | solution.py:15
  14.9 780.6 %all-reduce.7.cloned.1.call-start = ((), (), s32[]{:S(2)}) async-start(), calls=%async_computation | async-start | bytes 1179648
  575.3 2.2 copy-start.3
  581.4 1.8 copy-start.4
  583.1 2.2 copy-start.3
  590.7 1.8 copy-start.4
  592.5 2.2 copy-start.3
  600.1 1.8 copy-start.4
  601.8 2.2 copy-start.3
  609.4 1.8 copy-start.4
  611.2 2.2 copy-start.3
  618.8 1.8 copy-start.4
  620.5 2.2 copy-start.3
  628.1 1.8 copy-start.4
  634.3 2.2 copy-start
  639.3 1.8 copy-start.1
  641.2 2.2 copy-start
  646.1 1.8 copy-start.1
  648.0 2.2 copy-start
  652.9 1.8 copy-start.1
  654.8 2.2 copy-start
  659.8 1.8 copy-start.1
  661.6 2.2 copy-start
  666.6 1.8 copy-start.1
  668.4 2.2 copy-start
  673.4 1.8 copy-start.1
  675.2 2.5 copy-start.2
  677.7 2.6 copy-start.5
  680.3 2.6 copy-start.6
  710.4 28.6 %copy-start.7 = (u32[256]{0:T(256)S(1)}, u32[256]{0:T(256)}, u32[]{:S(2)}) copy-start(u32[256]{0:T(256)} %constant.84) | copy-start | bytes 3076
Sparse Core Ops, SparseCore 0:
  15.0 560.1 all-reduce.8
  739.2 56.3 all-reduce.6
where the time goes:
time: 805 us
  waiting for transfers between devices  576 us (72%)
  other arithmetic  110 us (14%)
  matrix products  56.2 us (7%)
  local copies, waits for them, and re-layouts  47.5 us (6%)
  between operations  14.7 us (2%)
    psum x1, waiting for transfers between devices, broadcast(): return lax.psum(block, axis)  520 us
    dot_general x2, matrix products, inverse_lags(): jnp.dot(joined.reshape(-1, shape[-1]), lag_basis, precision=lax.Precision...  56.2 us
    unnamed x3, waiting for transfers between devices  55.9 us
    add x12, other arithmetic, add_hour(): imag_part = totals[1] + (left_re * right_im - left_im * right_re)  47.8 us
    cos x1, other arithmetic, make_basis(): return jnp.concatenate([jnp.cos(angles), -jnp.sin(angles)], 0) * factor  40.2 us
    while x48, local copies, waits for them, and re-layouts  29.3 us
  transfers between devices with their start and end apart: 2, of which 2 were waited for; matrix products, arithmetic and copies ran while one was open for 5% of the time, Pallas kernels for 0%

commit v1 on v0

v1 whole, which is shorter than its diff:
```python
import functools
import math

import jax
import jax.numpy as jnp
import ml_dtypes
import numpy as np
from jax import lax
from jax.experimental import pallas as pl
from jax.experimental.pallas import tpu as pltpu
from jax.sharding import PartitionSpec as P

LAGS = 512
NW = 18000
STEPS = 2
HALF = LAGS // 2
LANES = 128
CORES = 2
WAYS = 4
DEPTH = 256


def tables(bins, hours):
    freqs = np.arange(bins, dtype=np.int64)[:, None]
    odd = 2 * np.arange(HALF, dtype=np.int64)[None, :] + 1
    angles = ((freqs * odd) % (2 * NW)).astype(np.float64) * (math.pi / NW)
    factor = 1.0 / math.sqrt(2.0 * bins * hours)
    parts = []
    for table in (np.cos(angles) * factor, np.sin(angles) * factor):
        head = table.astype(ml_dtypes.bfloat16)
        tail = (table - head.astype(np.float64)).astype(ml_dtypes.bfloat16)
        parts += [head, tail]
    basis = np.stack(parts, 0)
    turn = np.arange(bins, dtype=np.float64) * (math.pi / NW)
    turns = np.stack([np.cos(turn), np.sin(turn)], 0).astype(np.float32)
    turns = turns.reshape(2, bins // LANES, LANES).transpose(1, 0, 2)
    return basis, np.ascontiguousarray(turns)


def coords(index):
    return (index >> 4) & 3, (index >> 3) & 1, (index >> 1) & 3, index & 1


def pair_permute(value, shift):
    size = lax.axis_size("station")
    return lax.ppermute(value, "station", [(s, s ^ shift) for s in range(size)])


def along_x(value, distance):
    return pair_permute(value, distance << 4)


def along_y(value, distance):
    return pair_permute(value, distance << 1)


def pick(which, values):
    result = values[-1]
    for number in range(len(values) - 2, -1, -1):
        result = jnp.where(which == number, values[number], result)
    return result


def correlate_kernel(place, q0, q1, q2, q3, own, other, turns, basis, mine, theirs,
                     owner, local, lefts, acc):
    chunk = pl.program_id(0)
    last = pl.num_programs(0) - 1
    rows = own.shape[1]
    sub = rows // WAYS
    tiles = turns.shape[0]
    hours = 6
    first, second, window = place[0], place[1], place[2]

    def cross(which, slot):
        for part in range(2):
            tile = which * 2 + part
            lanes = slice(part * LANES, (part + 1) * LANES)
            turn = turns[tile]
            turn_re = jnp.broadcast_to(turn[0:1], (8, LANES))
            turn_im = jnp.broadcast_to(turn[1:2], (8, LANES))
            right = []
            for hour in range(hours):
                for comp in range(3):
                    at = (hour * 3 + comp) * 2 * tiles + tile * 2
                    x_re = local[pl.ds(at, 8, stride=rows), :]
                    x_im = local[pl.ds(at + 1, 8, stride=rows), :]
                    right.append((x_re * turn_re + x_im * turn_im, x_im * turn_re - x_re * turn_im))
            done = []
            for slot_i in range(WAYS):
                base = (window ^ slot_i) * rows + tile * 2
                for comp_i in range(3):
                    re = [None] * 3
                    im = [None] * 3
                    for hour in range(hours):
                        at = base + (hour * 3 + comp_i) * 2 * tiles
                        o_re = jnp.broadcast_to(owner[pl.ds(at, 1), :], (8, LANES))
                        o_im = jnp.broadcast_to(owner[pl.ds(at + 1, 1), :], (8, LANES))
                        for comp in range(3):
                            x_re, x_im = right[hour * 3 + comp]
                            new_re = o_re * x_re + o_im * x_im
                            new_im = o_re * x_im - o_im * x_re
                            re[comp] = new_re if hour == 0 else re[comp] + new_re
                            im[comp] = new_im if hour == 0 else im[comp] + new_im
                    done.append((re, im))
                    if len(done) == 2:
                        number = slot_i * 3 + comp_i - 1
                        where = slice(number * 24, number * 24 + 48)
                        for kind in range(2):
                            value = jnp.concatenate(done[0][kind] + done[1][kind], 0)
                            head = value.astype(jnp.bfloat16)
                            tail = (value - head.astype(jnp.float32)).astype(jnp.bfloat16)
                            lefts[slot, 2 * kind, where, lanes] = head
                            lefts[slot, 2 * kind + 1, where, lanes] = tail
                        done = []

    def transform(slot):
        for kind in range(2):
            head = lefts[slot, 2 * kind]
            tail = lefts[slot, 2 * kind + 1]
            table = basis[2 * kind]
            rest = basis[2 * kind + 1]
            dot = functools.partial(jnp.dot, preferred_element_type=jnp.float32)
            acc[kind] += dot(head, table) + dot(tail, table) + dot(head, rest)

    @pl.when(chunk == 0)
    def _():
        acc[...] = jnp.zeros_like(acc)
        for near, piece in enumerate((q0, q1, q2, q3)):
            base = (first ^ near) * rows
            for step in range(WAYS):
                at = pl.multiple_of(base + (second ^ step) * sub, 8)
                owner[pl.ds(at, sub), :] = piece[step].astype(jnp.float32)
        for near, source in enumerate((own, other)):
            for station in range(WAYS):
                at = (near * WAYS + station) * rows
                local[at:at + rows, :] = source[station].astype(jnp.float32)
        cross(0, 0)

    @pl.when(chunk < last)
    def _():
        cross(chunk + 1, lax.rem(chunk + 1, 2))
        transform(lax.rem(chunk, 2))

    @pl.when(chunk == last)
    def _():
        transform(lax.rem(chunk, 2))
        for kind in range(2):
            lanes = slice(kind * HALF, (kind + 1) * HALF)
            total = acc[kind].reshape(36, 8, HALF)
            mine[:, :, lanes] = total[:, 0:4]
            theirs[:, :, lanes] = total[:, 4:8]


def correlate(place, pieces, own, other, turns, basis):
    rows = own.shape[1]
    tiles = turns.shape[0] // CORES
    chunks = tiles * LANES // DEPTH

    def whole(shape):
        return pl.BlockSpec(shape, lambda k, s: (0,) * len(shape))

    spec = pltpu.PrefetchScalarGridSpec(
        num_scalar_prefetch=1,
        grid=(chunks,),
        in_specs=[whole(p.shape) for p in pieces]
        + [whole(own.shape), whole(other.shape)]
        + [pl.BlockSpec((tiles, 2, LANES), lambda k, s: (s[3], 0, 0)),
           pl.BlockSpec((4, DEPTH, HALF), lambda k, s: (0, s[3] * chunks + k, 0))],
        out_specs=[whole((36, 4, LAGS)), whole((36, 4, LAGS))],
        scratch_shapes=[
            pltpu.VMEM((WAYS * rows, LANES), jnp.float32),
            pltpu.VMEM((CORES * WAYS * rows, LANES), jnp.float32),
            pltpu.VMEM((2, 4, 288, DEPTH), jnp.bfloat16),
            pltpu.VMEM((2, 288, HALF), jnp.float32),
        ],
    )
    out = jax.ShapeDtypeStruct((36, 4, LAGS), jnp.float32)
    return pl.pallas_call(
        correlate_kernel,
        grid_spec=spec,
        out_shape=[out, out],
        compiler_params=pltpu.CompilerParams(vmem_limit_bytes=40 * 2**20),
        cost_estimate=pl.CostEstimate(flops=8 * 10**9, bytes_accessed=10**7, transcendentals=0),
    )(place, *pieces, own, other, turns, basis)


def finish_kernel(a0, a1, a2, a3, b0, b1, b2, b3, flip, out):
    for step, parts in enumerate(((a0, a1, a2, a3), (b0, b1, b2, b3))):
        total = (parts[0][...] + parts[1][...]) + (parts[2][...] + parts[3][...])
        even = total[:, :, 0:HALF]
        odd = total[:, :, HALF:LAGS]
        early = (even + odd).reshape(36, HALF)
        early = jnp.dot(early, flip[...], precision=lax.Precision.HIGHEST,
                        preferred_element_type=jnp.float32).reshape(9, 4, HALF)
        late = even - odd
        for a in range(3):
            for b in range(3):
                out[0, step, a, :, b, 0:HALF] = early[a * 3 + b]
                out[0, step, a, :, b, HALF:LAGS] = late[a * 3 + b]


def finish(parts, flip):
    return pl.pallas_call(
        finish_kernel,
        out_shape=jax.ShapeDtypeStruct((1, STEPS, 3, 4, 3, LAGS), jnp.float32),
        compiler_params=pltpu.CompilerParams(vmem_limit_bytes=16 * 2**20),
    )(*parts[0], *parts[1], flip)


def body(spectra, valid_mask, plan):
    windows = lax.axis_size("window")
    stations, hours, comps, _, bins = spectra.shape
    tiles = bins // LANES
    half = tiles // CORES
    used = hours * comps * half * 2
    rows = -(-used // 32) * 32
    x, z, y, core = coords(lax.axis_index("station"))
    window = lax.axis_index("window")

    masked = spectra * valid_mask.astype(jnp.bfloat16)[:, :, None, None, None]
    masked = masked.reshape(stations, hours * comps, 2, tiles, LANES).transpose(0, 1, 3, 2, 4)
    halves = []
    for number in range(CORES):
        piece = masked[:, :, number * half:(number + 1) * half].reshape(stations, used, LANES)
        halves.append(jnp.pad(piece, ((0, 0), (0, rows - used), (0, 0))))
    own = jnp.where(core == 0, halves[0], halves[1])
    other = pair_permute(jnp.where(core == 0, halves[1], halves[0]), 1)

    sub = rows // WAYS
    moves = ((along_x, along_y), (along_y, along_x))
    places = []
    small = []
    for step in range(STEPS):
        root_x, root_z, root_y, root_core = coords(plan[step])
        near_x, near_y = root_x ^ x, root_y ^ y
        first, second = ((near_x, near_y), (near_y, near_x))[step]
        go_first, go_second = moves[step]
        block = jnp.where(root_core == core, own, other)
        parts = [block[0]] + [go_first(block[d], d) for d in range(1, WAYS)]
        piece = pick(first, parts).reshape(WAYS, sub, LANES)
        parts = [piece[0]] + [go_second(piece[d], d) for d in range(1, WAYS)]
        small.append(pick(second, parts))
        places.append((first, second, root_z == z))
    both = jnp.stack(small, 0)
    across = pair_permute(both, 8)
    totals = []
    basis, turns = tables(bins, hours * windows)
    for step in range(STEPS):
        first, second, here = places[step]
        go_first, go_second = moves[step]
        mine = jnp.where(here, both[step], across[step])
        piece = jnp.stack([mine] + [go_second(mine, d) for d in range(1, WAYS)], 0)
        pieces = [piece] + [go_first(piece, d) for d in range(1, WAYS)]
        place = jnp.stack([first, second, window, core]).astype(jnp.int32)
        kept, given = correlate(place, pieces, own, other, jnp.asarray(turns), jnp.asarray(basis))
        total = (kept + pair_permute(given, 1)).reshape(windows, 9, 4, LAGS)
        totals.append([total[0]] + [
            lax.ppermute(total[d], "window", [(w, w ^ d) for w in range(windows)])
            for d in range(1, windows)])
    flip = jnp.asarray(np.eye(HALF, dtype=np.float32)[::-1].copy())
    return finish(totals, flip)


def solution(mesh):
    return jax.shard_map(
        body,
        mesh=mesh,
        in_specs=(P("station", "window", None, None, None), P("station", "window"), P()),
        out_specs=P("window", None, None, "station", None, None),
        check_vma=False,
    )
```

time: 805 us -> 114 us (0.14)
  waiting for transfers between devices: 576 us -> 17.7 us
  other arithmetic: 110 us -> 4.33 us
  matrix products: 56.2 us -> 0 us
  starting transfers between devices: 0.04 us -> 55.7 us
  local copies, waits for them, and re-layouts: 47.5 us -> 7.53 us
  Pallas kernels: 0 us -> 22.7 us
  between operations: 14.7 us -> 5.4 us
    psum x1 -> x0, waiting for transfers between devices: 520 us -> none  [broadcast(): return lax.psum(block, axis)]
    dot_general x2 -> x0, matrix products: 56.2 us -> none  [inverse_lags(): jnp.dot(joined.reshape(-1, shape[-1]), lag_basis, precision=lax.Precision...]
    unnamed x3 -> x0, waiting for transfers between devices: 55.9 us -> none
    ppermute x0 -> x34, starting transfers between devices: none -> 55.7 us  [the longest x28 41.9 us: pair_permute(): return lax.ppermute(value, 'station', [(s, s ^ shift) for s in range(size)])]
    add x12 -> x2, other arithmetic: 47.8 us -> 0.16 us  [body(): total = (kept + pair_permute(given, 1)).reshape(windows, 9, 4, LAGS)]
    while x52 -> x0, local copies, waits for them, and re-layouts: 41.4 us -> none
    cos x1 -> x0, other arithmetic: 40.2 us -> none  [make_basis(): return jnp.concatenate([jnp.cos(angles), -jnp.sin(angles)], 0) * factor]
    pallas_call x0 -> x3, Pallas kernels: none -> 22.7 us  [the longest x2 22.3 us: correlate(): pl.pallas_call(correlate_kernel, grid_spec=spec, out_shape=[out, out], co...]
  transfers between devices with their start and end apart: 2 -> 34, of which waited for: 2 -> 11; matrix products, arithmetic and copies ran while one was open for 5% -> 1% of each run, Pallas kernels for 0% -> 20%
where the time goes in v1:
time: 114 us; the launch traced here: 113 us
  starting transfers between devices  55.7 us (49%)
  Pallas kernels  22.7 us (20%)
  waiting for transfers between devices  17.7 us (16%)
  local copies, waits for them, and re-layouts  7.53 us (7%)
  between operations  5.4 us (5%)
  other arithmetic  4.33 us (4%)
    ppermute x28, starting transfers between devices, pair_permute(): return lax.ppermute(value, 'station', [(s, s ^ shift) for s in range(size)])  41.9 us
    pallas_call x2, Pallas kernels, correlate(): pl.pallas_call(correlate_kernel, grid_spec=spec, out_shape=[out, out], co...  22.3 us
    ppermute x6, starting transfers between devices, body(): lax.ppermute(total[d], 'window', [(w, w ^ d) for w in range(windows)])  13.8 us
    ppermute x28, waiting for transfers between devices, pair_permute(): return lax.ppermute(value, 'station', [(s, s ^ shift) for s in range(size)])  10.8 us
    ppermute x6, waiting for transfers between devices, body(): lax.ppermute(total[d], 'window', [(w, w ^ d) for w in range(windows)])  6.89 us
    unnamed x8, local copies, waits for them, and re-layouts  3.69 us
    mul x1, other arithmetic, body(): masked = spectra * valid_mask.astype(jnp.bfloat16)[:, :, None, None, None]  2.52 us
  transfers between devices with their start and end apart: 34, of which 11 were waited for; matrix products, arithmetic and copies ran while one was open for 1% of the time, Pallas kernels for 20%

profile of v1, /device:TPU:1, one launch (start us, length us, event | category | flops | bytes accessed | tf_op | source)
XLA Modules:
  0.0 113.4 jit_solution(1390253294009508047)
XLA Ops:
  0.0 0.7 convert_element_type.6
  0.7 2.5 %broadcast_multiply_fusion = bf16[4,6,3,2,4608]{4,3,2,1,0:T(2,128)(2,1)S(1)} fusion(bf16[4,6,3,2,4608]{4,3,2,1,0:T(2,128)(2,1)} %param.6, bf16[4,6]{1,0:T(4,128)(2,1)S(1)} %convert_element_type.6), kind=kLoop, calls=%fused_computation.4 | loop fusion | flops 663552 | bytes 2654256 | tf_op jit(solution)/shard_map/mul | solution.py:220
  3.2 0.9 reshape.74
  4.1 0.4 fusion.4
  4.6 0.5 copy.10
  5.1 0.5 copy.9
  5.6 0.2 broadcast_select_fusion.1
  5.8 3.3 %collective-permute-start = (bf16[4,672,128]{2,1,0:T(8,128)(2,1)S(1)}, bf16[4,672,128]{2,1,0:T(8,128)(2,1)S(1)}, u32[]{:S(2)}, u32[]{:S(2)}) collective-permute-start(bf16[4,672,128]{2,1,0:T(8,128)(2,1)S(1)} %broadcast_select_fusion.1), channel_id=1, source_target_pairs={{0,4},{4,0},{8,12},{12,8},{16,20},{20,16},{24,28},{28,24},{32,36},... | collective-permute-start | bytes 2064392 | tf_op jit(solution)/shard_map/ppermute | solution.py:46
  9.2 0.6 fusion.9
  13.6 0.3 broadcast_select_fusion
  14.1 2.2 %collective-permute-start.8 = (bf16[672,128]{1,0:T(8,128)(2,1)S(1)}, bf16[672,128]{1,0:T(8,128)(2,1)S(1)}, u32[]{:S(2)}, u32[]{:S(2)}) collective-permute-start(bf16[672,128]{1,0:T(8,128)(2,1)S(1)} %get-tuple-element.18), channel_id=1, source_target_pairs={{0,16},{4,20},{8,24},{12,28},{16,0},{20,4},{24,8},{28,12},{32,48},... | collective-permute-start | bytes 516104 | tf_op jit(solution)/shard_map/ppermute | solution.py:46
  16.2 1.7 %collective-permute-start.9 = (bf16[672,128]{1,0:T(8,128)(2,1)S(1)}, bf16[672,128]{1,0:T(8,128)(2,1)S(1)}, u32[]{:S(2)}, u32[]{:S(2)}) collective-permute-start(bf16[672,128]{1,0:T(8,128)(2,1)S(1)} %get-tuple-element.17), channel_id=1, source_target_pairs={{0,24},{4,28},{8,16},{12,20},{16,8},{20,12},{24,0},{28,4},{32,56},... | collective-permute-start | bytes 516104 | tf_op jit(solution)/shard_map/ppermute | solution.py:46
  18.1 2.0 %collective-permute-start.2 = (bf16[672,128]{1,0:T(8,128)(2,1)S(1)}, bf16[672,128]{1,0:T(8,128)(2,1)S(1)}, u32[]{:S(2)}, u32[]{:S(2)}) collective-permute-start(bf16[672,128]{1,0:T(8,128)(2,1)S(1)} %get-tuple-element.21), channel_id=1, source_target_pairs={{0,128},{4,132},{8,136},{12,140},{16,144},{20,148},{24,152},{28,15... | collective-permute-start | bytes 516104 | tf_op jit(solution)/shard_map/ppermute | solution.py:46
  20.1 1.9 %collective-permute-start.3 = (bf16[672,128]{1,0:T(8,128)(2,1)S(1)}, bf16[672,128]{1,0:T(8,128)(2,1)S(1)}, u32[]{:S(2)}, u32[]{:S(2)}) collective-permute-start(bf16[672,128]{1,0:T(8,128)(2,1)S(1)} %get-tuple-element.20), channel_id=1, source_target_pairs={{0,192},{4,196},{8,200},{12,204},{16,208},{20,212},{24,216},{28,22... | collective-permute-start | bytes 516104 | tf_op jit(solution)/shard_map/ppermute | solution.py:46
  22.0 2.1 %collective-permute-done.8 = bf16[672,128]{1,0:T(8,128)(2,1)S(1)} collective-permute-done((bf16[672,128]{1,0:T(8,128)(2,1)S(1)}, bf16[672,128]{1,0:T(8,128)(2,1)S(1)}, u32[]{:S(2)}, u32[]{:S(2)}) %collective-permute-start.8) | collective-permute-done | bytes 172064 | tf_op jit(solution)/shard_map/ppermute | solution.py:46
  24.1 2.6 %collective-permute-done.9 = bf16[672,128]{1,0:T(8,128)(2,1)S(1)} collective-permute-done((bf16[672,128]{1,0:T(8,128)(2,1)S(1)}, bf16[672,128]{1,0:T(8,128)(2,1)S(1)}, u32[]{:S(2)}, u32[]{:S(2)}) %collective-permute-start.9) | collective-permute-done | bytes 172064 | tf_op jit(solution)/shard_map/ppermute | solution.py:46
  26.7 1.3 %collective-permute-start.10 = (bf16[168,128]{1,0:T(8,128)(2,1)S(1)}, bf16[168,128]{1,0:T(8,128)(2,1)S(1)}, u32[]{:S(2)}, u32[]{:S(2)}) collective-permute-start(bf16[168,128]{1,0:T(8,128)(2,1)S(1)} %get-tuple-element.33), channel_id=1, source_target_pairs={{0,64},{4,68},{8,72},{12,76},{16,80},{20,84},{24,88},{28,92},{32,9... | collective-permute-start | bytes 129032 | tf_op jit(solution)/shard_map/ppermute | solution.py:46
  28.0 2.5 %collective-permute-start.11 = (bf16[168,128]{1,0:T(8,128)(2,1)S(1)}, bf16[168,128]{1,0:T(8,128)(2,1)S(1)}, u32[]{:S(2)}, u32[]{:S(2)}) collective-permute-start(bf16[168,128]{1,0:T(8,128)(2,1)S(1)} %get-tuple-element.32), channel_id=1, source_target_pairs={{0,128},{4,132},{8,136},{12,140},{16,144},{20,148},{24,152},{28,15... | collective-permute-start | bytes 129032 | tf_op jit(solution)/shard_map/ppermute | solution.py:46
  30.5 0.2 collective-permute-start.12
  30.9 3.0 %collective-permute-start.5 = (bf16[168,128]{1,0:T(8,128)(2,1)S(1)}, bf16[168,128]{1,0:T(8,128)(2,1)S(1)}, u32[]{:S(2)}, u32[]{:S(2)}) collective-permute-start(bf16[168,128]{1,0:T(8,128)(2,1)S(1)} %get-tuple-element.35), channel_id=1, source_target_pairs={{0,16},{4,20},{8,24},{12,28},{16,0},{20,4},{24,8},{28,12},{32,48},... | collective-permute-start | bytes 129032 | tf_op jit(solution)/shard_map/ppermute | solution.py:46
  33.9 0.8 collective-permute-start.6
  34.9 0.8 collective-permute-done.5
  35.7 2.8 %collective-permute-done.6 = bf16[168,128]{1,0:T(8,128)(2,1)S(1)} collective-permute-done((bf16[168,128]{1,0:T(8,128)(2,1)S(1)}, bf16[168,128]{1,0:T(8,128)(2,1)S(1)}, u32[]{:S(2)}, u32[]{:S(2)}) %collective-permute-start.6) | collective-permute-done | bytes 43040 | tf_op jit(solution)/shard_map/ppermute | solution.py:46
  38.6 2.1 %collective-permute-start.13 = (bf16[2,168,128]{2,1,0:T(8,128)(2,1)S(1)}, bf16[2,168,128]{2,1,0:T(8,128)(2,1)S(1)}, u32[]{:S(2)}, u32[]{:S(2)}) collective-permute-start(bf16[2,168,128]{2,1,0:T(8,128)(2,1)S(1)} %pad_maximum_fusion.2), channel_id=1, source_target_pairs={{0,32},{4,36},{8,40},{12,44},{16,48},{20,52},{24,56},{28,60},{32,0... | collective-permute-start | bytes 258056 | tf_op jit(solution)/shard_map/ppermute | solution.py:46
  41.9 0.6 collective-permute-done.13
  42.6 0.2 collective-permute-start.16
  42.9 3.0 %collective-permute-start.14 = (bf16[168,128]{1,0:T(8,128)(2,1)S(1)}, bf16[168,128]{1,0:T(8,128)(2,1)S(1)}, u32[]{:S(2)}, u32[]{:S(2)}) collective-permute-start(bf16[168,128]{1,0:T(8,128)(2,1)S(1)} %get-tuple-element.38), channel_id=1, source_target_pairs={{0,8},{4,12},{8,0},{12,4},{16,24},{20,28},{24,16},{28,20},{32,40},... | collective-permute-start | bytes 129032 | tf_op jit(solution)/shard_map/ppermute | solution.py:46
  46.0 0.7 collective-permute-start.26
  46.8 2.5 %collective-permute-start.24 = (bf16[168,128]{1,0:T(8,128)(2,1)S(1)}, bf16[168,128]{1,0:T(8,128)(2,1)S(1)}, u32[]{:S(2)}, u32[]{:S(2)}) collective-permute-start(bf16[168,128]{1,0:T(8,128)(2,1)S(1)} %get-tuple-element.37), channel_id=1, source_target_pairs={{0,64},{4,68},{8,72},{12,76},{16,80},{20,84},{24,88},{28,92},{32,9... | collective-permute-start | bytes 129032 | tf_op jit(solution)/shard_map/ppermute | solution.py:46
  49.4 2.1 %collective-permute-start.18 = (bf16[4,168,128]{2,1,0:T(8,128)(2,1)S(1)}, bf16[4,168,128]{2,1,0:T(8,128)(2,1)S(1)}, u32[]{:S(2)}, u32[]{:S(2)}) collective-permute-start(bf16[4,168,128]{2,1,0:T(8,128)(2,1)S(1)} %pad_maximum_fusion.q0), channel_id=1, source_target_pairs={{0,128},{4,132},{8,136},{12,140},{16,144},{20,148},{24,152},{28,15... | collective-permute-start | bytes 516104 | tf_op jit(solution)/shard_map/ppermute | solution.py:46
  51.6 1.7 %collective-permute-start.19 = (bf16[4,168,128]{2,1,0:T(8,128)(2,1)S(1)}, bf16[4,168,128]{2,1,0:T(8,128)(2,1)S(1)}, u32[]{:S(2)}, u32[]{:S(2)}) collective-permute-start(bf16[4,168,128]{2,1,0:T(8,128)(2,1)S(1)} %pad_maximum_fusion.q0), channel_id=1, source_target_pairs={{0,192},{4,196},{8,200},{12,204},{16,208},{20,212},{24,216},{28,22... | collective-permute-start | bytes 516104 | tf_op jit(solution)/shard_map/ppermute | solution.py:46
  53.5 1.8 %collective-permute-start.28 = (bf16[4,168,128]{2,1,0:T(8,128)(2,1)S(1)}, bf16[4,168,128]{2,1,0:T(8,128)(2,1)S(1)}, u32[]{:S(2)}, u32[]{:S(2)}) collective-permute-start(bf16[4,168,128]{2,1,0:T(8,128)(2,1)S(1)} %pad_maximum_fusion.1.q0), channel_id=1, source_target_pairs={{0,16},{4,20},{8,24},{12,28},{16,0},{20,4},{24,8},{28,12},{32,48},... | collective-permute-start | bytes 516104 | tf_op jit(solution)/shard_map/ppermute | solution.py:46
  55.3 2.0 %collective-permute-start.29 = (bf16[4,168,128]{2,1,0:T(8,128)(2,1)S(1)}, bf16[4,168,128]{2,1,0:T(8,128)(2,1)S(1)}, u32[]{:S(2)}, u32[]{:S(2)}) collective-permute-start(bf16[4,168,128]{2,1,0:T(8,128)(2,1)S(1)} %pad_maximum_fusion.1.q0), channel_id=1, source_target_pairs={{0,24},{4,28},{8,16},{12,20},{16,8},{20,12},{24,0},{28,4},{32,56},... | collective-permute-start | bytes 516104 | tf_op jit(solution)/shard_map/ppermute | solution.py:46
  57.3 1.6 %collective-permute-done.19.q3 = bf16[4,168,128]{2,1,0:T(8,128)(2,1)S(1)} collective-permute-done((bf16[4,168,128]{2,1,0:T(8,128)(2,1)S(1)}, bf16[4,168,128]{2,1,0:T(8,128)(2,1)S(1)}, u32[]{:S(2)}, u32[]{:S(2)}) %collective-permute-start.19) | collective-permute-done | bytes 172064 | tf_op jit(solution)/shard_map/ppermute | solution.py:46
  59.0 3.7 %copy-done.1 = bf16[4,4608,256]{2,1,0:T(8,128)(2,1)S(1)} copy-done((bf16[4,4608,256]{2,1,0:T(8,128)(2,1)S(1)}, bf16[4,4608,256]{2,1,0:T(8,128)(2,1)}, u32[]{:S(2)}) %copy-start.1) | copy-done | bytes 9437208
  62.6 11.2 %shard_map.64 = (f32[36,4,512]{2,1,0:T(4,128)S(1)}, f32[36,4,512]{2,1,0:T(4,128)S(1)}) custom-call(s32[4]{0:T(128)S(1)} %add_add_fusion.place, bf16[4,168,128]{2,1,0:T(8,128)(2,1)S(1)} %pad_maximum_fusion.q0, bf16[4,168,128]{2,1,0:T(8,128)(2,1)S(1)} %collective-permute-done.17.q1, bf16[4,168,128]{2,1,0:T(8,128)(2,1)S(1)} %collective-permute-done.18.q2, ...), custom_call_target="tpu_custom_call" | custom-call | flops 8000000000 | bytes 10000000 | tf_op jit(solution)/shard_map/pallas_call | solution.py:178
  73.8 6.0 %collective-permute-start.20 = (f32[36,4,512]{2,1,0:T(4,128)S(1)}, f32[36,4,512]{2,1,0:T(4,128)S(1)}, u32[]{:S(2)}, u32[]{:S(2)}) collective-permute-start(f32[36,4,512]{2,1,0:T(4,128)S(1)} %get-tuple-element.10), channel_id=1, source_target_pairs={{0,4},{4,0},{8,12},{12,8},{16,20},{20,16},{24,28},{28,24},{32,36},... | collective-permute-start | bytes 884744 | tf_op jit(solution)/shard_map/ppermute | solution.py:46
  79.8 11.2 %shard_map.65 = (f32[36,4,512]{2,1,0:T(4,128)S(1)}, f32[36,4,512]{2,1,0:T(4,128)S(1)}) custom-call(s32[4]{0:T(128)S(1)} %add_add_fusion.1.place, bf16[4,168,128]{2,1,0:T(8,128)(2,1)S(1)} %pad_maximum_fusion.1.q0, bf16[4,168,128]{2,1,0:T(8,128)(2,1)S(1)} %collective-permute-done.27.q1, bf16[4,168,128]{2,1,0:T(8,128)(2,1)S(1)} %collective-permute-done.28.q2, ...), custom_call_target="tpu_custom_call" | custom-call | flops 8000000000 | bytes 10000000 | tf_op jit(solution)/shard_map/pallas_call | solution.py:178
  91.0 0.3 collective-permute-start.30
  91.4 3.1 %collective-permute-start.21 = (f32[9,4,512]{2,1,0:T(4,128)S(1)}, f32[9,4,512]{2,1,0:T(4,128)S(1)}, u32[]{:S(2)}, u32[]{:S(2)}) collective-permute-start(f32[9,4,512]{2,1,0:T(4,128)S(1)} %get-tuple-element.29), channel_id=1, source_target_pairs={{0,1},{1,0},{2,3},{3,2},{4,5},{5,4},{6,7},{7,6},{8,9},{9,8},{10,11... | collective-permute-start | bytes 221192 | tf_op jit(solution)/shard_map/ppermute | solution.py:258
  94.5 5.0 %collective-permute-start.22 = (f32[9,4,512]{2,1,0:T(4,128)S(1)}, f32[9,4,512]{2,1,0:T(4,128)S(1)}, u32[]{:S(2)}, u32[]{:S(2)}) collective-permute-start(f32[9,4,512]{2,1,0:T(4,128)S(1)} %get-tuple-element.28), channel_id=1, source_target_pairs={{0,2},{1,3},{2,0},{3,1},{4,6},{5,7},{6,4},{7,5},{8,10},{9,11},{10,... | collective-permute-start | bytes 221192 | tf_op jit(solution)/shard_map/ppermute | solution.py:258
  99.6 1.3 %collective-permute-start.31 = (f32[9,4,512]{2,1,0:T(4,128)S(1)}, f32[9,4,512]{2,1,0:T(4,128)S(1)}, u32[]{:S(2)}, u32[]{:S(2)}) collective-permute-start(f32[9,4,512]{2,1,0:T(4,128)S(1)} %get-tuple-element.25), channel_id=1, source_target_pairs={{0,1},{1,0},{2,3},{3,2},{4,5},{5,4},{6,7},{7,6},{8,9},{9,8},{10,11... | collective-permute-start | bytes 221192 | tf_op jit(solution)/shard_map/ppermute | solution.py:258
  100.9 4.5 %collective-permute-start.32 = (f32[9,4,512]{2,1,0:T(4,128)S(1)}, f32[9,4,512]{2,1,0:T(4,128)S(1)}, u32[]{:S(2)}, u32[]{:S(2)}) collective-permute-start(f32[9,4,512]{2,1,0:T(4,128)S(1)} %get-tuple-element.24), channel_id=1, source_target_pairs={{0,2},{1,3},{2,0},{3,1},{4,6},{5,7},{6,4},{7,5},{8,10},{9,11},{10,... | collective-permute-start | bytes 221192 | tf_op jit(solution)/shard_map/ppermute | solution.py:258
  105.4 0.2 collective-permute-done.23.a3
  105.5 4.6 %collective-permute-done.31.b1 = f32[9,4,512]{2,1,0:T(4,128)S(1)} collective-permute-done((f32[9,4,512]{2,1,0:T(4,128)S(1)}, f32[9,4,512]{2,1,0:T(4,128)S(1)}, u32[]{:S(2)}, u32[]{:S(2)}) %collective-permute-start.31) | collective-permute-done | bytes 73760 | tf_op jit(solution)/shard_map/ppermute | solution.py:258
  110.2 2.1 %collective-permute-done.33.b3 = f32[9,4,512]{2,1,0:T(4,128)S(1)} collective-permute-done((f32[9,4,512]{2,1,0:T(4,128)S(1)}, f32[9,4,512]{2,1,0:T(4,128)S(1)}, u32[]{:S(2)}, u32[]{:S(2)}) %collective-permute-start.33) | collective-permute-done | bytes 73760 | tf_op jit(solution)/shard_map/ppermute | solution.py:258
  112.3 0.4 shard_map.66
  112.7 0.7 copy.11
  (60 shorter events, 1.7 us)
Async XLA Ops:
  5.6 3.5 %copy-start.3 = (s32[2]{0:T(128)S(1)}, s32[2]{0:T(128)}, u32[]{:S(2)}) copy-start(s32[2]{0:T(128)} %param.8) | copy-start | bytes 28
  5.8 7.8 %collective-permute-start = (bf16[4,672,128]{2,1,0:T(8,128)(2,1)S(1)}, bf16[4,672,128]{2,1,0:T(8,128)(2,1)S(1)}, u32[]{:S(2)}, u32[]{:S(2)}) collective-permute-start(bf16[4,672,128]{2,1,0:T(8,128)(2,1)S(1)} %broadcast_select_fusion.1), channel_id=1, source_target_pairs={{0,4},{4,0},{8,12},{12,8},{16,20},{20,16},{24,28},{28,24},{32,36},... | collective-permute-start | bytes 2064392 | tf_op jit(solution)/shard_map/ppermute | solution.py:46
  14.0 6.1 %collective-permute-start.7 = (bf16[672,128]{1,0:T(8,128)(2,1)S(1)}, bf16[672,128]{1,0:T(8,128)(2,1)S(1)}, u32[]{:S(2)}, u32[]{:S(2)}) collective-permute-start(bf16[672,128]{1,0:T(8,128)(2,1)S(1)} %get-tuple-element.19), channel_id=1, source_target_pairs={{0,8},{4,12},{8,0},{12,4},{16,24},{20,28},{24,16},{28,20},{32,40},... | collective-permute-start | bytes 516104 | tf_op jit(solution)/shard_map/ppermute | solution.py:46
  14.1 10.0 %collective-permute-start.8 = (bf16[672,128]{1,0:T(8,128)(2,1)S(1)}, bf16[672,128]{1,0:T(8,128)(2,1)S(1)}, u32[]{:S(2)}, u32[]{:S(2)}) collective-permute-start(bf16[672,128]{1,0:T(8,128)(2,1)S(1)} %get-tuple-element.18), channel_id=1, source_target_pairs={{0,16},{4,20},{8,24},{12,28},{16,0},{20,4},{24,8},{28,12},{32,48},... | collective-permute-start | bytes 516104 | tf_op jit(solution)/shard_map/ppermute | solution.py:46
  16.2 10.4 %collective-permute-start.9 = (bf16[672,128]{1,0:T(8,128)(2,1)S(1)}, bf16[672,128]{1,0:T(8,128)(2,1)S(1)}, u32[]{:S(2)}, u32[]{:S(2)}) collective-permute-start(bf16[672,128]{1,0:T(8,128)(2,1)S(1)} %get-tuple-element.17), channel_id=1, source_target_pairs={{0,24},{4,28},{8,16},{12,20},{16,8},{20,12},{24,0},{28,4},{32,56},... | collective-permute-start | bytes 516104 | tf_op jit(solution)/shard_map/ppermute | solution.py:46
  18.0 12.5 %collective-permute-start.1 = (bf16[672,128]{1,0:T(8,128)(2,1)S(1)}, bf16[672,128]{1,0:T(8,128)(2,1)S(1)}, u32[]{:S(2)}, u32[]{:S(2)}) collective-permute-start(bf16[672,128]{1,0:T(8,128)(2,1)S(1)} %get-tuple-element.22), channel_id=1, source_target_pairs={{0,64},{4,68},{8,72},{12,76},{16,80},{20,84},{24,88},{28,92},{32,9... | collective-permute-start | bytes 516104 | tf_op jit(solution)/shard_map/ppermute | solution.py:46
  18.1 12.6 %collective-permute-start.2 = (bf16[672,128]{1,0:T(8,128)(2,1)S(1)}, bf16[672,128]{1,0:T(8,128)(2,1)S(1)}, u32[]{:S(2)}, u32[]{:S(2)}) collective-permute-start(bf16[672,128]{1,0:T(8,128)(2,1)S(1)} %get-tuple-element.21), channel_id=1, source_target_pairs={{0,128},{4,132},{8,136},{12,140},{16,144},{20,148},{24,152},{28,15... | collective-permute-start | bytes 516104 | tf_op jit(solution)/shard_map/ppermute | solution.py:46
  20.1 10.6 %collective-permute-start.3 = (bf16[672,128]{1,0:T(8,128)(2,1)S(1)}, bf16[672,128]{1,0:T(8,128)(2,1)S(1)}, u32[]{:S(2)}, u32[]{:S(2)}) collective-permute-start(bf16[672,128]{1,0:T(8,128)(2,1)S(1)} %get-tuple-element.20), channel_id=1, source_target_pairs={{0,192},{4,196},{8,200},{12,204},{16,208},{20,212},{24,216},{28,22... | collective-permute-start | bytes 516104 | tf_op jit(solution)/shard_map/ppermute | solution.py:46
  26.7 7.1 %collective-permute-start.10 = (bf16[168,128]{1,0:T(8,128)(2,1)S(1)}, bf16[168,128]{1,0:T(8,128)(2,1)S(1)}, u32[]{:S(2)}, u32[]{:S(2)}) collective-permute-start(bf16[168,128]{1,0:T(8,128)(2,1)S(1)} %get-tuple-element.33), channel_id=1, source_target_pairs={{0,64},{4,68},{8,72},{12,76},{16,80},{20,84},{24,88},{28,92},{32,9... | collective-permute-start | bytes 129032 | tf_op jit(solution)/shard_map/ppermute | solution.py:46
  28.0 6.7 %collective-permute-start.11 = (bf16[168,128]{1,0:T(8,128)(2,1)S(1)}, bf16[168,128]{1,0:T(8,128)(2,1)S(1)}, u32[]{:S(2)}, u32[]{:S(2)}) collective-permute-start(bf16[168,128]{1,0:T(8,128)(2,1)S(1)} %get-tuple-element.32), channel_id=1, source_target_pairs={{0,128},{4,132},{8,136},{12,140},{16,144},{20,148},{24,152},{28,15... | collective-permute-start | bytes 129032 | tf_op jit(solution)/shard_map/ppermute | solution.py:46
  30.5 28.5 %copy-start.2 = (f32[36,2,128]{2,1,0:T(2,128)S(1)}, f32[36,2,128]{2,1,0:T(2,128)}, u32[]{:S(2)}) copy-start(f32[36,2,128]{2,1,0:T(2,128)} %constant.44.clone.turns) | copy-start | bytes 110596
  30.5 4.4 %collective-permute-start.12 = (bf16[168,128]{1,0:T(8,128)(2,1)S(1)}, bf16[168,128]{1,0:T(8,128)(2,1)S(1)}, u32[]{:S(2)}, u32[]{:S(2)}) collective-permute-start(bf16[168,128]{1,0:T(8,128)(2,1)S(1)} %get-tuple-element.31), channel_id=1, source_target_pairs={{0,192},{4,196},{8,200},{12,204},{16,208},{20,212},{24,216},{28,22... | collective-permute-start | bytes 129032 | tf_op jit(solution)/shard_map/ppermute | solution.py:46
  30.8 4.1 %collective-permute-start.4 = (bf16[168,128]{1,0:T(8,128)(2,1)S(1)}, bf16[168,128]{1,0:T(8,128)(2,1)S(1)}, u32[]{:S(2)}, u32[]{:S(2)}) collective-permute-start(bf16[168,128]{1,0:T(8,128)(2,1)S(1)} %get-tuple-element.36), channel_id=1, source_target_pairs={{0,8},{4,12},{8,0},{12,4},{16,24},{20,28},{24,16},{28,20},{32,40},... | collective-permute-start | bytes 129032 | tf_op jit(solution)/shard_map/ppermute | solution.py:46
  30.9 4.9 %collective-permute-start.5 = (bf16[168,128]{1,0:T(8,128)(2,1)S(1)}, bf16[168,128]{1,0:T(8,128)(2,1)S(1)}, u32[]{:S(2)}, u32[]{:S(2)}) collective-permute-start(bf16[168,128]{1,0:T(8,128)(2,1)S(1)} %get-tuple-element.35), channel_id=1, source_target_pairs={{0,16},{4,20},{8,24},{12,28},{16,0},{20,4},{24,8},{28,12},{32,48},... | collective-permute-start | bytes 129032 | tf_op jit(solution)/shard_map/ppermute | solution.py:46
  33.9 4.7 %collective-permute-start.6 = (bf16[168,128]{1,0:T(8,128)(2,1)S(1)}, bf16[168,128]{1,0:T(8,128)(2,1)S(1)}, u32[]{:S(2)}, u32[]{:S(2)}) collective-permute-start(bf16[168,128]{1,0:T(8,128)(2,1)S(1)} %get-tuple-element.34), channel_id=1, source_target_pairs={{0,24},{4,28},{8,16},{12,20},{16,8},{20,12},{24,0},{28,4},{32,56},... | collective-permute-start | bytes 129032 | tf_op jit(solution)/shard_map/ppermute | solution.py:46
  38.6 3.9 %collective-permute-start.13 = (bf16[2,168,128]{2,1,0:T(8,128)(2,1)S(1)}, bf16[2,168,128]{2,1,0:T(8,128)(2,1)S(1)}, u32[]{:S(2)}, u32[]{:S(2)}) collective-permute-start(bf16[2,168,128]{2,1,0:T(8,128)(2,1)S(1)} %pad_maximum_fusion.2), channel_id=1, source_target_pairs={{0,32},{4,36},{8,40},{12,44},{16,48},{20,52},{24,56},{28,60},{32,0... | collective-permute-start | bytes 258056 | tf_op jit(solution)/shard_map/ppermute | solution.py:46
  42.6 4.2 %collective-permute-start.16 = (bf16[168,128]{1,0:T(8,128)(2,1)S(1)}, bf16[168,128]{1,0:T(8,128)(2,1)S(1)}, u32[]{:S(2)}, u32[]{:S(2)}) collective-permute-start(bf16[168,128]{1,0:T(8,128)(2,1)S(1)} %get-tuple-element.38), channel_id=1, source_target_pairs={{0,24},{4,28},{8,16},{12,20},{16,8},{20,12},{24,0},{28,4},{32,56},... | collective-permute-start | bytes 129032 | tf_op jit(solution)/shard_map/ppermute | solution.py:46
  42.8 6.5 %collective-permute-start.15 = (bf16[168,128]{1,0:T(8,128)(2,1)S(1)}, bf16[168,128]{1,0:T(8,128)(2,1)S(1)}, u32[]{:S(2)}, u32[]{:S(2)}) collective-permute-start(bf16[168,128]{1,0:T(8,128)(2,1)S(1)} %get-tuple-element.38), channel_id=1, source_target_pairs={{0,16},{4,20},{8,24},{12,28},{16,0},{20,4},{24,8},{28,12},{32,48},... | collective-permute-start | bytes 129032 | tf_op jit(solution)/shard_map/ppermute | solution.py:46
  42.9 6.4 %collective-permute-start.14 = (bf16[168,128]{1,0:T(8,128)(2,1)S(1)}, bf16[168,128]{1,0:T(8,128)(2,1)S(1)}, u32[]{:S(2)}, u32[]{:S(2)}) collective-permute-start(bf16[168,128]{1,0:T(8,128)(2,1)S(1)} %get-tuple-element.38), channel_id=1, source_target_pairs={{0,8},{4,12},{8,0},{12,4},{16,24},{20,28},{24,16},{28,20},{32,40},... | collective-permute-start | bytes 129032 | tf_op jit(solution)/shard_map/ppermute | solution.py:46
  46.0 5.6 %collective-permute-start.26 = (bf16[168,128]{1,0:T(8,128)(2,1)S(1)}, bf16[168,128]{1,0:T(8,128)(2,1)S(1)}, u32[]{:S(2)}, u32[]{:S(2)}) collective-permute-start(bf16[168,128]{1,0:T(8,128)(2,1)S(1)} %get-tuple-element.37), channel_id=1, source_target_pairs={{0,192},{4,196},{8,200},{12,204},{16,208},{20,212},{24,216},{28,22... | collective-permute-start | bytes 129032 | tf_op jit(solution)/shard_map/ppermute | solution.py:46
  46.6 6.7 %collective-permute-start.25 = (bf16[168,128]{1,0:T(8,128)(2,1)S(1)}, bf16[168,128]{1,0:T(8,128)(2,1)S(1)}, u32[]{:S(2)}, u32[]{:S(2)}) collective-permute-start(bf16[168,128]{1,0:T(8,128)(2,1)S(1)} %get-tuple-element.37), channel_id=1, source_target_pairs={{0,128},{4,132},{8,136},{12,140},{16,144},{20,148},{24,152},{28,15... | collective-permute-start | bytes 129032 | tf_op jit(solution)/shard_map/ppermute | solution.py:46
  46.8 6.6 %collective-permute-start.24 = (bf16[168,128]{1,0:T(8,128)(2,1)S(1)}, bf16[168,128]{1,0:T(8,128)(2,1)S(1)}, u32[]{:S(2)}, u32[]{:S(2)}) collective-permute-start(bf16[168,128]{1,0:T(8,128)(2,1)S(1)} %get-tuple-element.37), channel_id=1, source_target_pairs={{0,64},{4,68},{8,72},{12,76},{16,80},{20,84},{24,88},{28,92},{32,9... | collective-permute-start | bytes 129032 | tf_op jit(solution)/shard_map/ppermute | solution.py:46
  49.3 6.0 %collective-permute-start.17 = (bf16[4,168,128]{2,1,0:T(8,128)(2,1)S(1)}, bf16[4,168,128]{2,1,0:T(8,128)(2,1)S(1)}, u32[]{:S(2)}, u32[]{:S(2)}) collective-permute-start(bf16[4,168,128]{2,1,0:T(8,128)(2,1)S(1)} %pad_maximum_fusion.q0), channel_id=1, source_target_pairs={{0,64},{4,68},{8,72},{12,76},{16,80},{20,84},{24,88},{28,92},{32,9... | collective-permute-start | bytes 516104 | tf_op jit(solution)/shard_map/ppermute | solution.py:46
  49.4 7.9 %collective-permute-start.18 = (bf16[4,168,128]{2,1,0:T(8,128)(2,1)S(1)}, bf16[4,168,128]{2,1,0:T(8,128)(2,1)S(1)}, u32[]{:S(2)}, u32[]{:S(2)}) collective-permute-start(bf16[4,168,128]{2,1,0:T(8,128)(2,1)S(1)} %pad_maximum_fusion.q0), channel_id=1, source_target_pairs={{0,128},{4,132},{8,136},{12,140},{16,144},{20,148},{24,152},{28,15... | collective-permute-start | bytes 516104 | tf_op jit(solution)/shard_map/ppermute | solution.py:46
  51.6 7.4 %collective-permute-start.19 = (bf16[4,168,128]{2,1,0:T(8,128)(2,1)S(1)}, bf16[4,168,128]{2,1,0:T(8,128)(2,1)S(1)}, u32[]{:S(2)}, u32[]{:S(2)}) collective-permute-start(bf16[4,168,128]{2,1,0:T(8,128)(2,1)S(1)} %pad_maximum_fusion.q0), channel_id=1, source_target_pairs={{0,192},{4,196},{8,200},{12,204},{16,208},{20,212},{24,216},{28,22... | collective-permute-start | bytes 516104 | tf_op jit(solution)/shard_map/ppermute | solution.py:46
  53.4 26.4 %collective-permute-start.27 = (bf16[4,168,128]{2,1,0:T(8,128)(2,1)S(1)}, bf16[4,168,128]{2,1,0:T(8,128)(2,1)S(1)}, u32[]{:S(2)}, u32[]{:S(2)}) collective-permute-start(bf16[4,168,128]{2,1,0:T(8,128)(2,1)S(1)} %pad_maximum_fusion.1.q0), channel_id=1, source_target_pairs={{0,8},{4,12},{8,0},{12,4},{16,24},{20,28},{24,16},{28,20},{32,40},... | collective-permute-start | bytes 516104 | tf_op jit(solution)/shard_map/ppermute | solution.py:46
  53.5 26.3 %collective-permute-start.28 = (bf16[4,168,128]{2,1,0:T(8,128)(2,1)S(1)}, bf16[4,168,128]{2,1,0:T(8,128)(2,1)S(1)}, u32[]{:S(2)}, u32[]{:S(2)}) collective-permute-start(bf16[4,168,128]{2,1,0:T(8,128)(2,1)S(1)} %pad_maximum_fusion.1.q0), channel_id=1, source_target_pairs={{0,16},{4,20},{8,24},{12,28},{16,0},{20,4},{24,8},{28,12},{32,48},... | collective-permute-start | bytes 516104 | tf_op jit(solution)/shard_map/ppermute | solution.py:46
  55.3 24.5 %collective-permute-start.29 = (bf16[4,168,128]{2,1,0:T(8,128)(2,1)S(1)}, bf16[4,168,128]{2,1,0:T(8,128)(2,1)S(1)}, u32[]{:S(2)}, u32[]{:S(2)}) collective-permute-start(bf16[4,168,128]{2,1,0:T(8,128)(2,1)S(1)} %pad_maximum_fusion.1.q0), channel_id=1, source_target_pairs={{0,24},{4,28},{8,16},{12,20},{16,8},{20,12},{24,0},{28,4},{32,56},... | collective-permute-start | bytes 516104 | tf_op jit(solution)/shard_map/ppermute | solution.py:46
  59.0 3.7 %copy-start.1 = (bf16[4,4608,256]{2,1,0:T(8,128)(2,1)S(1)}, bf16[4,4608,256]{2,1,0:T(8,128)(2,1)}, u32[]{:S(2)}) copy-start(bf16[4,4608,256]{2,1,0:T(8,128)(2,1)} %constant.45.clone.basis) | copy-start | bytes 28311556
  73.8 17.5 %collective-permute-start.20 = (f32[36,4,512]{2,1,0:T(4,128)S(1)}, f32[36,4,512]{2,1,0:T(4,128)S(1)}, u32[]{:S(2)}, u32[]{:S(2)}) collective-permute-start(f32[36,4,512]{2,1,0:T(4,128)S(1)} %get-tuple-element.10), channel_id=1, source_target_pairs={{0,4},{4,0},{8,12},{12,8},{16,20},{20,16},{24,28},{28,24},{32,36},... | collective-permute-start | bytes 884744 | tf_op jit(solution)/shard_map/ppermute | solution.py:46
  91.0 8.6 %collective-permute-start.30 = (f32[36,4,512]{2,1,0:T(4,128)S(1)}, f32[36,4,512]{2,1,0:T(4,128)S(1)}, u32[]{:S(2)}, u32[]{:S(2)}) collective-permute-start(f32[36,4,512]{2,1,0:T(4,128)S(1)} %get-tuple-element.12), channel_id=1, source_target_pairs={{0,4},{4,0},{8,12},{12,8},{16,20},{20,16},{24,28},{28,24},{32,36},... | collective-permute-start | bytes 884744 | tf_op jit(solution)/shard_map/ppermute | solution.py:46
  91.3 21.0 %copy-start = (f32[256,256]{1,0:T(8,128)S(1)}, f32[256,256]{1,0:T(8,128)}, u32[]{:S(2)}) copy-start(f32[256,256]{1,0:T(8,128)} %constant.46.clone.flip) | copy-start | bytes 786436
  91.4 14.0 %collective-permute-start.21 = (f32[9,4,512]{2,1,0:T(4,128)S(1)}, f32[9,4,512]{2,1,0:T(4,128)S(1)}, u32[]{:S(2)}, u32[]{:S(2)}) collective-permute-start(f32[9,4,512]{2,1,0:T(4,128)S(1)} %get-tuple-element.29), channel_id=1, source_target_pairs={{0,1},{1,0},{2,3},{3,2},{4,5},{5,4},{6,7},{7,6},{8,9},{9,8},{10,11... | collective-permute-start | bytes 221192 | tf_op jit(solution)/shard_map/ppermute | solution.py:258
  94.5 10.9 %collective-permute-start.22 = (f32[9,4,512]{2,1,0:T(4,128)S(1)}, f32[9,4,512]{2,1,0:T(4,128)S(1)}, u32[]{:S(2)}, u32[]{:S(2)}) collective-permute-start(f32[9,4,512]{2,1,0:T(4,128)S(1)} %get-tuple-element.28), channel_id=1, source_target_pairs={{0,2},{1,3},{2,0},{3,1},{4,6},{5,7},{6,4},{7,5},{8,10},{9,11},{10,... | collective-permute-start | bytes 221192 | tf_op jit(solution)/shard_map/ppermute | solution.py:258
  99.5 6.0 %collective-permute-start.23 = (f32[9,4,512]{2,1,0:T(4,128)S(1)}, f32[9,4,512]{2,1,0:T(4,128)S(1)}, u32[]{:S(2)}, u32[]{:S(2)}) collective-permute-start(f32[9,4,512]{2,1,0:T(4,128)S(1)} %get-tuple-element.27), channel_id=1, source_target_pairs={{0,3},{1,2},{2,1},{3,0},{4,7},{5,6},{6,5},{7,4},{8,11},{9,10},{10,... | collective-permute-start | bytes 221192 | tf_op jit(solution)/shard_map/ppermute | solution.py:258
  99.6 10.5 %collective-permute-start.31 = (f32[9,4,512]{2,1,0:T(4,128)S(1)}, f32[9,4,512]{2,1,0:T(4,128)S(1)}, u32[]{:S(2)}, u32[]{:S(2)}) collective-permute-start(f32[9,4,512]{2,1,0:T(4,128)S(1)} %get-tuple-element.25), channel_id=1, source_target_pairs={{0,1},{1,0},{2,3},{3,2},{4,5},{5,4},{6,7},{7,6},{8,9},{9,8},{10,11... | collective-permute-start | bytes 221192 | tf_op jit(solution)/shard_map/ppermute | solution.py:258
  100.9 9.3 %collective-permute-start.32 = (f32[9,4,512]{2,1,0:T(4,128)S(1)}, f32[9,4,512]{2,1,0:T(4,128)S(1)}, u32[]{:S(2)}, u32[]{:S(2)}) collective-permute-start(f32[9,4,512]{2,1,0:T(4,128)S(1)} %get-tuple-element.24), channel_id=1, source_target_pairs={{0,2},{1,3},{2,0},{3,1},{4,6},{5,7},{6,4},{7,5},{8,10},{9,11},{10,... | collective-permute-start | bytes 221192 | tf_op jit(solution)/shard_map/ppermute | solution.py:258
  105.4 6.9 %collective-permute-start.33 = (f32[9,4,512]{2,1,0:T(4,128)S(1)}, f32[9,4,512]{2,1,0:T(4,128)S(1)}, u32[]{:S(2)}, u32[]{:S(2)}) collective-permute-start(f32[9,4,512]{2,1,0:T(4,128)S(1)} %get-tuple-element.23), channel_id=1, source_target_pairs={{0,3},{1,2},{2,1},{3,0},{4,7},{5,6},{6,5},{7,4},{8,11},{9,10},{10,... | collective-permute-start | bytes 221192 | tf_op jit(solution)/shard_map/ppermute | solution.py:258

commit v2 on v0

v2 whole, which is shorter than its diff:
```python
import functools
import math

import jax
import jax.numpy as jnp
import ml_dtypes
import numpy as np
from jax import lax
from jax.experimental import pallas as pl
from jax.experimental.pallas import tpu as pltpu
from jax.sharding import PartitionSpec as P

LAGS = 512
NW = 18000
STEPS = 2
HALF = LAGS // 2
LANES = 128
CORES = 2
WAYS = 4
DEPTH = 256


def tables(bins, hours):
    freqs = np.arange(bins, dtype=np.int64)[:, None]
    odd = 2 * np.arange(HALF, dtype=np.int64)[None, :] + 1
    angles = ((freqs * odd) % (2 * NW)).astype(np.float64) * (math.pi / NW)
    factor = 1.0 / math.sqrt(2.0 * bins * hours)
    parts = []
    for table in (np.cos(angles) * factor, np.sin(angles) * factor):
        head = table.astype(ml_dtypes.bfloat16)
        tail = (table - head.astype(np.float64)).astype(ml_dtypes.bfloat16)
        parts += [head, tail]
    basis = np.stack(parts, 0).reshape(2, 2, CORES, -1, DEPTH, HALF)
    basis = np.ascontiguousarray(basis.transpose(2, 3, 0, 1, 4, 5))
    turn = np.arange(bins, dtype=np.float64) * (math.pi / NW)
    turns = np.stack([np.cos(turn), np.sin(turn)], 0).astype(np.float32)
    turns = turns.reshape(2, CORES, bins // LANES // CORES, LANES).transpose(1, 2, 0, 3)
    return basis, np.ascontiguousarray(turns)


def coords(index):
    return (index >> 4) & 3, (index >> 3) & 1, (index >> 1) & 3, index & 1


def pair_permute(value, even, odd=None):
    size = lax.axis_size("station")
    shifts = (even, even if odd is None else odd)
    return lax.ppermute(value, "station", [(s, s ^ shifts[s & 1]) for s in range(size)])


def along_first(value, distance):
    return pair_permute(value, distance << 4, distance << 1)


def along_second(value, distance):
    return pair_permute(value, distance << 1, distance << 4)


def pick(which, values):
    result = values[-1]
    for number in range(len(values) - 2, -1, -1):
        result = jnp.where(which == number, values[number], result)
    return result


def turn_kernel(own, other, turns, out, local):
    rows = own.shape[1]
    tiles = out.shape[0]
    for near, source in enumerate((own, other)):
        for station in range(WAYS):
            at = (near * WAYS + station) * rows
            local[at:at + rows, :] = source[station].astype(jnp.float32)

    def one(tile, carry):
        turn = turns[tile]
        turn_re = jnp.broadcast_to(turn[0:1], (8, LANES))
        turn_im = jnp.broadcast_to(turn[1:2], (8, LANES))
        for part in range(18):
            at = part * 2 * tiles + tile * 2
            x_re = local[pl.ds(at, 8, stride=rows), :]
            x_im = local[pl.ds(at + 1, 8, stride=rows), :]
            out[tile, 2 * part] = x_re * turn_re + x_im * turn_im
            out[tile, 2 * part + 1] = x_im * turn_re - x_re * turn_im
        return carry

    lax.fori_loop(0, tiles, one, 0)


def turn_right(own, other, turns):
    tiles = turns.shape[0]
    rows = own.shape[1]
    return pl.pallas_call(
        turn_kernel,
        in_specs=[pl.BlockSpec(memory_space=pltpu.VMEM)] * 3,
        out_specs=pl.BlockSpec(memory_space=pltpu.VMEM),
        out_shape=jax.ShapeDtypeStruct((tiles, 36, 8, LANES), jnp.float32),
        scratch_shapes=[pltpu.VMEM((8 * rows, LANES), jnp.float32)],
        compiler_params=pltpu.CompilerParams(vmem_limit_bytes=16 * 2**20),
        cost_estimate=pl.CostEstimate(flops=10**7, bytes_accessed=10**6, transcendentals=0),
    )(own, other, turns)


def correlate_kernel(slots, place, own, other, right, basis,
                     mine, theirs, owner, lefts, acc, tables, sems):
    rows = own.shape[1]
    sub = rows // WAYS
    tiles = right.shape[0]
    chunks = tiles * LANES // DEPTH
    window, core = place[2], place[3]
    size = WAYS * rows

    def bring(chunk):
        return pltpu.make_async_copy(basis.at[core, chunk], tables.at[chunk], sems.at[chunk])

    for chunk in range(chunks):
        bring(chunk).start()

    def cross(chunk, slot):
        for part in range(2):
            tile = chunk * 2 + part
            lanes = part * LANES
            turned = [right[tile, n] for n in range(36)]
            sums = [turned[2 * n] + turned[2 * n + 1] for n in range(18)]
            done = []
            for number in range(STEPS * len(slots) * 3):
                step, rest = divmod(number, len(slots) * 3)
                slot_i, comp_i = divmod(rest, 3)
                start = step * size + (window ^ slots[slot_i]) * rows + tile * 2
                parts = [None] * 3
                for hour in range(6):
                    at = start + (hour * 3 + comp_i) * 2 * tiles
                    o_re = jnp.broadcast_to(owner[pl.ds(at, 1), :], (8, LANES))
                    o_im = jnp.broadcast_to(owner[pl.ds(at + 1, 1), :], (8, LANES))
                    o_sum = o_re + o_im
                    o_dif = o_re - o_im
                    for comp in range(3):
                        at = hour * 3 + comp
                        new = (o_re * sums[at], o_sum * turned[2 * at], o_dif * turned[2 * at + 1])
                        parts[comp] = new if hour == 0 else [p + n for p, n in zip(parts[comp], new)]
                done.append(([p[0] - p[2] for p in parts], [p[0] - p[1] for p in parts]))
                if len(done) == 2:
                    where = slice((number - 1) * 24, (number + 1) * 24)
                    for kind in range(2):
                        value = jnp.concatenate(done[0][kind] + done[1][kind], 0)
                        head = value.astype(jnp.bfloat16)
                        tail = (value - head.astype(jnp.float32)).astype(jnp.bfloat16)
                        lefts[slot, kind, where, lanes:lanes + LANES] = head
                        lefts[slot, kind, where, DEPTH + lanes:DEPTH + lanes + LANES] = tail
                    done = []

    def transform(chunk, slot):
        dot = functools.partial(jnp.dot, preferred_element_type=jnp.float32)
        for kind in range(2):
            head = lefts[slot, kind, :, 0:DEPTH]
            tail = lefts[slot, kind, :, DEPTH:2 * DEPTH]
            table = tables[chunk, kind, 0]
            rest = tables[chunk, kind, 1]
            acc[kind] += dot(head, table) + dot(tail, table) + dot(head, rest)

    acc[...] = jnp.zeros_like(acc)
    for step, pieces in ((core, own), (1 - core, other)):
        first, second = place[4 * step], place[4 * step + 1]
        for near in range(WAYS):
            piece = pieces[near].astype(jnp.float32)
            for number in range(WAYS):
                at = pl.multiple_of(step * size + (first ^ near) * rows + (second ^ number) * sub, 8)
                owner[pl.ds(at, sub), :] = piece[number * sub:(number + 1) * sub]
    cross(0, 0)

    def one(chunk, carry):
        slot = lax.rem(chunk, 2)
        bring(chunk).wait()
        transform(chunk, slot)
        cross(chunk + 1, 1 - slot)
        return carry

    lax.fori_loop(0, chunks - 1, one, 0)
    slot = (chunks - 1) % 2
    bring(chunks - 1).wait()
    transform(chunks - 1, slot)
    for kind in range(2):
        lanes = slice(kind * HALF, (kind + 1) * HALF)
        total = acc[kind].reshape(STEPS, len(slots), 9, 8, HALF)
        for step in range(STEPS):
            here = slice(step * 9, step * 9 + 9)
            mine[:, here, :, lanes] = total[step, :, :, 0:4]
            theirs[:, here, :, lanes] = total[step, :, :, 4:8]


def correlate(slots, place, own, other, right, basis):
    rows = own.shape[1]
    chunks = basis.shape[1]
    lines = STEPS * len(slots) * 72
    out = jax.ShapeDtypeStruct((len(slots), STEPS * 9, 4, LAGS), jnp.float32)
    return pl.pallas_call(
        functools.partial(correlate_kernel, slots),
        in_specs=[pl.BlockSpec(memory_space=pltpu.SMEM)]
        + [pl.BlockSpec(memory_space=pltpu.VMEM)] * 3
        + [pl.BlockSpec(memory_space=pl.ANY)],
        out_specs=[pl.BlockSpec(memory_space=pltpu.VMEM)] * 2,
        out_shape=[out, out],
        scratch_shapes=[
            pltpu.VMEM((STEPS * WAYS * rows, LANES), jnp.float32),
            pltpu.VMEM((2, 2, lines, 2 * DEPTH), jnp.bfloat16),
            pltpu.VMEM((2, lines, HALF), jnp.float32),
            pltpu.VMEM(basis.shape[1:], jnp.bfloat16),
            pltpu.SemaphoreType.DMA((chunks,)),
        ],
        compiler_params=pltpu.CompilerParams(vmem_limit_bytes=50 * 2**20),
        cost_estimate=pl.CostEstimate(flops=lines * 3 * 10**7, bytes_accessed=10**6, transcendentals=0),
    )(place, own, other, right, basis)


def finish_kernel(m0, t0, p1, p2, p3, flip, out):
    total = (m0[0] + t0[0]) + (p1[...] + (p2[...] + p3[...]))
    even = total[:, :, 0:HALF]
    odd = total[:, :, HALF:LAGS]
    early = jnp.dot((even + odd).reshape(72, HALF), flip[...], precision=lax.Precision.HIGHEST,
                    preferred_element_type=jnp.float32)
    out[0, :, :, :, :, 0:HALF] = early.reshape(STEPS, 3, 3, 4, HALF)
    out[0, :, :, :, :, HALF:LAGS] = (even - odd).reshape(STEPS, 3, 3, 4, HALF)


def finish(parts, flip):
    return pl.pallas_call(
        finish_kernel,
        out_shape=jax.ShapeDtypeStruct((1, STEPS, 3, 3, 4, LAGS), jnp.float32),
        compiler_params=pltpu.CompilerParams(vmem_limit_bytes=16 * 2**20),
    )(*parts, flip)


def pad_rows(value, rows):
    widths = [(0, 0)] * value.ndim
    widths[-2] = (0, rows - value.shape[-2])
    return jnp.pad(value, widths)


def body(spectra, valid_mask, plan):
    windows = lax.axis_size("window")
    stations, hours, comps, _, bins = spectra.shape
    tiles = bins // LANES
    half = tiles // CORES
    used = hours * comps * half * 2
    rows = -(-used // 32) * 32
    sub = rows // WAYS
    x, z, y, core = coords(lax.axis_index("station"))
    window = lax.axis_index("window")
    basis, turns = tables(bins, hours * windows)

    masked = spectra * valid_mask.astype(jnp.bfloat16)[:, :, None, None, None]
    masked = masked.reshape(stations, hours * comps, 2, tiles, LANES).transpose(0, 1, 3, 2, 4)
    halves = [masked[:, :, n * half:(n + 1) * half].reshape(stations, used, LANES)
              for n in range(CORES)]
    whole = pad_rows(jnp.stack(halves), rows)
    across = pair_permute(whole, 1)
    own = jnp.where(core == 0, whole[0], whole[1])
    other = jnp.where(core == 0, across[0], across[1])
    turns = lax.dynamic_index_in_dim(jnp.asarray(turns), core, 0, keepdims=False)
    right = turn_right(own, other, turns)

    roots = lax.optimization_barrier(jnp.broadcast_to(plan[:, None], (STEPS, LANES)))
    lane = lax.iota(jnp.int32, LANES)
    near = []
    for step in range(STEPS):
        root_x, _, root_y, _ = coords(roots[step])
        near.append((root_x ^ x, root_y ^ y))
    mine = jnp.where(core == 0, roots[0], roots[1])
    first = jnp.where(core == 0, near[0][0], near[1][1])
    second = jnp.where(core == 0, near[0][1], near[1][0])
    _, root_z, _, root_core = coords(mine)
    place = pick(lane, [near[0][0], near[0][1], jnp.broadcast_to(window, (LANES,)),
                        jnp.broadcast_to(core, (LANES,)), near[1][1], near[1][0]])
    block = jnp.where(root_core == core, whole, across)
    parts = [block[:, 0]] + [along_first(block[:, d], d) for d in range(1, WAYS)]
    piece = pick(first, parts)
    cuts = [piece[:, d * sub:(d + 1) * sub] for d in range(WAYS)]
    parts = [cuts[0]] + [along_second(cuts[d], d) for d in range(1, WAYS)]
    small, right = lax.optimization_barrier((pick(second, parts), right))
    small = jnp.where(root_z == z, small, pair_permute(small, 8))
    piece = jnp.concatenate([small] + [along_second(small, d) for d in range(1, WAYS)], 1)
    pieces = [piece] + [along_first(piece, d) for d in range(1, WAYS)]
    own = jnp.stack([jnp.where(core == 0, p[0], p[1]) for p in pieces])
    other = pair_permute(jnp.stack([jnp.where(core == 0, p[1], p[0]) for p in pieces]), 1)
    basis = jnp.asarray(basis)
    kept, given = correlate((1, 2, 3), place, own, other, right, basis)
    total = kept + pair_permute(given, 1)
    place, total = lax.optimization_barrier((place, total))
    parts = [lax.ppermute(total[d - 1], "window", [(w, w ^ d) for w in range(windows)])
             for d in range(1, windows)]
    kept, given = correlate((0,), place, own, other, right, basis)
    given, parts = lax.optimization_barrier((given, parts))
    flip = jnp.asarray(np.eye(HALF, dtype=np.float32)[::-1].copy())
    return finish([kept, pair_permute(given, 1)] + parts, flip).transpose(0, 1, 2, 4, 3, 5)


def solution(mesh):
    return jax.shard_map(
        body,
        mesh=mesh,
        in_specs=(P("station", "window", None, None, None), P("station", "window"), P()),
        out_specs=P("window", None, None, "station", None, None),
        check_vma=False,
    )
```

time: 805 us -> 102 us (0.13)
  waiting for transfers between devices: 576 us -> 38.1 us
  other arithmetic: 110 us -> 6.83 us
  matrix products: 56.2 us -> 0 us
  local copies, waits for them, and re-layouts: 47.5 us -> 2.61 us
  starting transfers between devices: 0.04 us -> 33.6 us
  Pallas kernels: 0 us -> 20.5 us
  between operations: 14.7 us -> 0.22 us
    psum x1 -> x0, waiting for transfers between devices: 520 us -> none  [broadcast(): return lax.psum(block, axis)]
    dot_general x2 -> x0, matrix products: 56.2 us -> none  [inverse_lags(): jnp.dot(joined.reshape(-1, shape[-1]), lag_basis, precision=lax.Precision...]
    unnamed x3 -> x0, waiting for transfers between devices: 55.9 us -> none
    add x12 -> x1, other arithmetic: 47.8 us -> 0.12 us  [body(): total = kept + pair_permute(given, 1)]
    while x52 -> x0, local copies, waits for them, and re-layouts: 41.4 us -> none
    cos x1 -> x0, other arithmetic: 40.2 us -> none  [make_basis(): return jnp.concatenate([jnp.cos(angles), -jnp.sin(angles)], 0) * factor]
    ppermute x0 -> x20, waiting for transfers between devices: none -> 38.1 us  [the longest x17 30 us: pair_permute(): lax.ppermute(value, 'station', [(s, s ^ shifts[s & 1]) for s in range(siz...]
    ppermute x0 -> x20, starting transfers between devices: none -> 33.6 us  [the longest x17 25.1 us: pair_permute(): lax.ppermute(value, 'station', [(s, s ^ shifts[s & 1]) for s in range(siz...]
  transfers between devices with their start and end apart: 2 -> 20, of which waited for: 2 -> 16; matrix products, arithmetic and copies ran while one was open for 5% -> 2% of each run, Pallas kernels for 0% -> 8%
where the time goes in v2:
time: 102 us
  waiting for transfers between devices  38.1 us (37%)
  starting transfers between devices  33.6 us (33%)
  Pallas kernels  20.5 us (20%)
  other arithmetic  6.83 us (7%)
  local copies, waits for them, and re-layouts  2.61 us (3%)
    ppermute x17, waiting for transfers between devices, pair_permute(): lax.ppermute(value, 'station', [(s, s ^ shifts[s & 1]) for s in range(siz...  30 us
    ppermute x17, starting transfers between devices, pair_permute(): lax.ppermute(value, 'station', [(s, s ^ shifts[s & 1]) for s in range(siz...  25.1 us
    pallas_call x2, Pallas kernels, correlate(): pl.pallas_call(functools.partial(correlate_kernel, slots), in_specs=[pl.B...  17.8 us
    ppermute x3, starting transfers between devices, body(): lax.ppermute(total[d - 1], 'window', [(w, w ^ d) for w in range(windows)])  8.47 us
    ppermute x3, waiting for transfers between devices, body(): lax.ppermute(total[d - 1], 'window', [(w, w ^ d) for w in range(windows)])  8.19 us
    mul x1, other arithmetic, body(): masked = spectra * valid_mask.astype(jnp.bfloat16)[:, :, None, None, None]  2.52 us
  transfers between devices with their start and end apart: 20, of which 16 were waited for; matrix products, arithmetic and copies ran while one was open for 2% of the time, Pallas kernels for 8%

profile of v2, /device:TPU:1, one launch (start us, length us, event | category | flops | bytes accessed | tf_op | source)
XLA Modules:
  0.0 101.9 jit_solution(6674478653956019107)
XLA Ops:
  0.0 0.7 convert_element_type.5
  0.7 2.5 %broadcast_multiply_fusion = bf16[4,6,3,2,4608]{4,3,2,1,0:T(2,128)(2,1)S(1)} fusion(bf16[4,6,3,2,4608]{4,3,2,1,0:T(2,128)(2,1)} %param.6, bf16[4,6]{1,0:T(4,128)(2,1)S(1)} %convert_element_type.5), kind=kLoop, calls=%fused_computation.11 | loop fusion | flops 663552 | bytes 2654256 | tf_op jit(solution)/shard_map/mul | solution.py:250
  3.2 0.9 reshape.45
  4.1 0.4 fusion.6
  4.6 0.5 copy.8
  5.1 0.5 copy.9
  5.6 1.2 %fusion.2 = bf16[2,4,672,128]{3,2,0,1:T(8,128)(2,1)} fusion(bf16[1,4,648,128]{3,2,0,1:T(8,128)(2,1)S(1)} %bitcast.49, bf16[1,4,648,128]{3,2,0,1:T(8,128)(2,1)S(1)} %bitcast.47), kind=kLoop, calls=%fused_computation.3 | loop fusion | flops 4816896 | bytes 2703360 | tf_op jit(solution)/shard_map/stack | solution.py:254
  6.8 3.2 %collective-permute-start = (bf16[2,4,672,128]{3,2,0,1:T(8,128)(2,1)}, bf16[2,4,672,128]{3,2,0,1:T(8,128)(2,1)S(1)}, u32[]{:S(2)}, u32[]{:S(2)}) collective-permute-start(bf16[2,4,672,128]{3,2,0,1:T(8,128)(2,1)} %fusion.2), channel_id=1, source_target_pairs={{0,4},{4,0},{8,12},{12,8},{16,20},{20,16},{24,28},{28,24},{32,36},... | collective-permute-start | bytes 4128776 | tf_op jit(solution)/shard_map/ppermute | solution.py:48
  10.2 2.8 %collective-permute-done = bf16[2,4,672,128]{3,2,0,1:T(8,128)(2,1)S(1)} collective-permute-done((bf16[2,4,672,128]{3,2,0,1:T(8,128)(2,1)}, bf16[2,4,672,128]{3,2,0,1:T(8,128)(2,1)S(1)}, u32[]{:S(2)}, u32[]{:S(2)}) %collective-permute-start) | collective-permute-done | bytes 1376288 | tf_op jit(solution)/shard_map/ppermute | solution.py:48
  13.1 0.4 broadcast_select_fusion
  13.5 1.1 %collective-permute-start.3 = (bf16[2,672,128]{2,1,0:T(8,128)(2,1)S(1)}, bf16[2,672,128]{2,1,0:T(8,128)(2,1)S(1)}, u32[]{:S(2)}, u32[]{:S(2)}) collective-permute-start(bf16[2,672,128]{2,1,0:T(8,128)(2,1)S(1)} %get-tuple-element.35), channel_id=1, source_target_pairs={{0,192},{4,28},{8,200},{12,20},{16,208},{20,12},{24,216},{28,4},{3... | collective-permute-start | bytes 1032200 | tf_op jit(solution)/shard_map/ppermute | solution.py:48
  14.9 1.9 %collective-permute-start.1 = (bf16[2,672,128]{2,1,0:T(8,128)(2,1)S(1)}, bf16[2,672,128]{2,1,0:T(8,128)(2,1)S(1)}, u32[]{:S(2)}, u32[]{:S(2)}) collective-permute-start(bf16[2,672,128]{2,1,0:T(8,128)(2,1)S(1)} %get-tuple-element.37), channel_id=1, source_target_pairs={{0,64},{4,12},{8,72},{12,4},{16,80},{20,28},{24,88},{28,20},{32,96... | collective-permute-start | bytes 1032200 | tf_op jit(solution)/shard_map/ppermute | solution.py:48
  16.9 1.4 %fusion.4.own = bf16[4,672,128]{2,1,0:T(8,128)(2,1)S(1)} fusion(bf16[2,4,672,128]{3,2,0,1:T(8,128)(2,1)} %fusion.2, pred[]{:T(512)S(6)} %eq.69), kind=kLoop, calls=%fused_computation.8 | loop fusion | flops 344064 | bytes 2064385 | tf_op jit(solution)/shard_map/jit(_where)/select_n | solution.py:256
  18.2 6.6 %collective-permute-done.3 = bf16[2,672,128]{2,1,0:T(8,128)(2,1)S(1)} collective-permute-done((bf16[2,672,128]{2,1,0:T(8,128)(2,1)S(1)}, bf16[2,672,128]{2,1,0:T(8,128)(2,1)S(1)}, u32[]{:S(2)}, u32[]{:S(2)}) %collective-permute-start.3) | collective-permute-done | bytes 344096 | tf_op jit(solution)/shard_map/ppermute | solution.py:48
  24.9 0.6 collective-permute-done.1
  25.6 1.0 collective-permute-start.6
  26.6 0.5 collective-permute-start.5
  27.1 1.8 %collective-permute-start.4 = (bf16[2,168,128]{2,1,0:T(8,128)(2,1)S(1)}, bf16[2,168,128]{2,1,0:T(8,128)(2,1)S(1)}, u32[]{:S(2)}, u32[]{:S(2)}) collective-permute-start(bf16[2,168,128]{2,1,0:T(8,128)(2,1)S(1)} %get-tuple-element.51), channel_id=1, source_target_pairs={{0,8},{4,68},{8,0},{12,76},{16,24},{20,84},{24,16},{28,92},{32,40}... | collective-permute-start | bytes 258056 | tf_op jit(solution)/shard_map/ppermute | solution.py:48
  29.1 1.8 %shard_map.64.right = f32[18,36,8,128]{3,2,1,0:T(8,128)S(1)} custom-call(bf16[4,672,128]{2,1,0:T(8,128)(2,1)S(1)} %fusion.4.own, bf16[4,672,128]{2,1,0:T(8,128)(2,1)S(1)} %fusion.3.other, f32[18,2,128]{2,1,0:T(2,128)S(1)} %dynamic-slice_bitcast_fusion.turns), custom_call_target="tpu_custom_call" | custom-call | flops 10000000 | bytes 1000000 | tf_op jit(solution)/shard_map/pallas_call | solution.py:92
  30.9 0.6 collective-permute-done.5
  31.5 0.6 collective-permute-done.4
  32.1 1.1 %collective-permute-start.7 = (bf16[2,168,128]{2,1,0:T(8,128)(2,1)S(1)}, bf16[2,168,128]{2,1,0:T(8,128)(2,1)S(1)}, u32[]{:S(2)}, u32[]{:S(2)}) collective-permute-start(bf16[2,168,128]{2,1,0:T(8,128)(2,1)S(1)} %slice_select_fusion.2), channel_id=1, source_target_pairs={{0,32},{4,36},{8,40},{12,44},{16,48},{20,52},{24,56},{28,60},{32,0... | collective-permute-start | bytes 258056 | tf_op jit(solution)/shard_map/ppermute | solution.py:48
  33.2 2.3 %collective-permute-done.7 = bf16[2,168,128]{2,1,0:T(8,128)(2,1)S(1)} collective-permute-done((bf16[2,168,128]{2,1,0:T(8,128)(2,1)S(1)}, bf16[2,168,128]{2,1,0:T(8,128)(2,1)S(1)}, u32[]{:S(2)}, u32[]{:S(2)}) %collective-permute-start.7) | collective-permute-done | bytes 86048 | tf_op jit(solution)/shard_map/ppermute | solution.py:48
  35.5 1.3 %collective-permute-start.10 = (bf16[2,168,128]{2,1,0:T(8,128)(2,1)S(1)}, bf16[2,168,128]{2,1,0:T(8,128)(2,1)S(1)}, u32[]{:S(2)}, u32[]{:S(2)}) collective-permute-start(bf16[2,168,128]{2,1,0:T(8,128)(2,1)S(1)} %broadcast_select_fusion.9), channel_id=1, source_target_pairs={{0,24},{4,196},{8,16},{12,204},{16,8},{20,212},{24,0},{28,220},{32... | collective-permute-start | bytes 258056 | tf_op jit(solution)/shard_map/ppermute | solution.py:48
  36.8 0.9 collective-permute-start.9
  37.7 1.2 %collective-permute-start.8 = (bf16[2,168,128]{2,1,0:T(8,128)(2,1)S(1)}, bf16[2,168,128]{2,1,0:T(8,128)(2,1)S(1)}, u32[]{:S(2)}, u32[]{:S(2)}) collective-permute-start(bf16[2,168,128]{2,1,0:T(8,128)(2,1)S(1)} %broadcast_select_fusion.9), channel_id=1, source_target_pairs={{0,8},{4,68},{8,0},{12,76},{16,24},{20,84},{24,16},{28,92},{32,40}... | collective-permute-start | bytes 258056 | tf_op jit(solution)/shard_map/ppermute | solution.py:48
  38.9 1.3 %collective-permute-done.10 = bf16[2,168,128]{2,1,0:T(8,128)(2,1)S(1)} collective-permute-done((bf16[2,168,128]{2,1,0:T(8,128)(2,1)S(1)}, bf16[2,168,128]{2,1,0:T(8,128)(2,1)S(1)}, u32[]{:S(2)}, u32[]{:S(2)}) %collective-permute-start.10) | collective-permute-done | bytes 86048 | tf_op jit(solution)/shard_map/ppermute | solution.py:48
  40.2 1.5 %collective-permute-done.9 = bf16[2,168,128]{2,1,0:T(8,128)(2,1)S(1)} collective-permute-done((bf16[2,168,128]{2,1,0:T(8,128)(2,1)S(1)}, bf16[2,168,128]{2,1,0:T(8,128)(2,1)S(1)}, u32[]{:S(2)}, u32[]{:S(2)}) %collective-permute-start.9) | collective-permute-done | bytes 86048 | tf_op jit(solution)/shard_map/ppermute | solution.py:48
  41.7 2.7 %collective-permute-start.12 = (bf16[2,672,128]{2,1,0:T(8,128)(2,1)S(1)}, bf16[2,672,128]{2,1,0:T(8,128)(2,1)S(1)}, u32[]{:S(2)}, u32[]{:S(2)}) collective-permute-start(bf16[2,672,128]{2,1,0:T(8,128)(2,1)S(1)} %pad_maximum_fusion.2), channel_id=1, source_target_pairs={{0,128},{4,20},{8,136},{12,28},{16,144},{20,4},{24,152},{28,12},{3... | collective-permute-start | bytes 1032200 | tf_op jit(solution)/shard_map/ppermute | solution.py:48
  44.4 0.4 collective-permute-start.11
  44.8 0.5 collective-permute-start.13
  45.3 5.8 %collective-permute-done.12 = bf16[2,672,128]{2,1,0:T(8,128)(2,1)S(1)} collective-permute-done((bf16[2,672,128]{2,1,0:T(8,128)(2,1)S(1)}, bf16[2,672,128]{2,1,0:T(8,128)(2,1)S(1)}, u32[]{:S(2)}, u32[]{:S(2)}) %collective-permute-start.12) | collective-permute-done | bytes 344096 | tf_op jit(solution)/shard_map/ppermute | solution.py:48
  51.2 2.9 %collective-permute-done.11 = bf16[2,672,128]{2,1,0:T(8,128)(2,1)S(1)} collective-permute-done((bf16[2,672,128]{2,1,0:T(8,128)(2,1)S(1)}, bf16[2,672,128]{2,1,0:T(8,128)(2,1)S(1)}, u32[]{:S(2)}, u32[]{:S(2)}) %collective-permute-start.11) | collective-permute-done | bytes 344096 | tf_op jit(solution)/shard_map/ppermute | solution.py:48
  54.1 0.8 collective-permute-done.13
  55.0 6.1 %collective-permute-start.14 = (bf16[4,672,128]{2,1,0:T(8,128)(2,1)S(1)}, bf16[4,672,128]{2,1,0:T(8,128)(2,1)S(1)}, u32[]{:S(2)}, u32[]{:S(2)}) collective-permute-start(bf16[4,672,128]{2,1,0:T(8,128)(2,1)S(1)} %pad_maximum_fusion.1), channel_id=1, source_target_pairs={{0,4},{4,0},{8,12},{12,8},{16,20},{20,16},{24,28},{28,24},{32,36},... | collective-permute-start | bytes 2064392 | tf_op jit(solution)/shard_map/ppermute | solution.py:48
  61.3 1.7 %collective-permute-done.14.other = bf16[4,672,128]{2,1,0:T(8,128)(2,1)S(1)} collective-permute-done((bf16[4,672,128]{2,1,0:T(8,128)(2,1)S(1)}, bf16[4,672,128]{2,1,0:T(8,128)(2,1)S(1)}, u32[]{:S(2)}, u32[]{:S(2)}) %collective-permute-start.14) | collective-permute-done | bytes 688160 | tf_op jit(solution)/shard_map/ppermute | solution.py:48
  62.9 11.7 %shard_map.65 = (f32[3,18,4,512]{3,2,1,0:T(4,128)S(1)}, f32[3,18,4,512]{3,2,1,0:T(4,128)S(1)}) custom-call(s32[128]{0:T(128)S(1)} %compare_select_fusion.4.place, bf16[4,672,128]{2,1,0:T(8,128)(2,1)S(1)} %pad_maximum_fusion.own, bf16[4,672,128]{2,1,0:T(8,128)(2,1)S(1)} %collective-permute-done.14.other, f32[18,36,8,128]{3,2,1,0:T(8,128)} %copy-done, ...), custom_call_target="tpu_custom_call" | custom-call | flops 12960000000 | bytes 1000000 | tf_op jit(solution)/shard_map/pallas_call | solution.py:195
  74.6 0.5 collective-permute-start.15
  75.1 1.4 %collective-permute-done.15 = f32[3,18,4,512]{3,2,1,0:T(4,128)S(1)} collective-permute-done((f32[3,18,4,512]{3,2,1,0:T(4,128)S(1)}, f32[3,18,4,512]{3,2,1,0:T(4,128)S(1)}, u32[]{:S(2)}, u32[]{:S(2)}) %collective-permute-start.15) | collective-permute-done | bytes 442400 | tf_op jit(solution)/shard_map/ppermute | solution.py:48
  76.7 6.3 %collective-permute-start.18 = (f32[18,4,512]{2,1,0:T(4,128)S(1)}, f32[18,4,512]{2,1,0:T(4,128)S(1)}, u32[]{:S(2)}, u32[]{:S(2)}) collective-permute-start(f32[18,4,512]{2,1,0:T(4,128)S(1)} %get-tuple-element.38), channel_id=1, source_target_pairs={{0,3},{1,2},{2,1},{3,0},{4,7},{5,6},{6,5},{7,4},{8,11},{9,10},{10,... | collective-permute-start | bytes 442376 | tf_op jit(solution)/shard_map/ppermute | solution.py:288
  82.9 1.0 collective-permute-start.17
  83.9 1.2 %collective-permute-start.16 = (f32[18,4,512]{2,1,0:T(4,128)S(1)}, f32[18,4,512]{2,1,0:T(4,128)S(1)}, u32[]{:S(2)}, u32[]{:S(2)}) collective-permute-start(f32[18,4,512]{2,1,0:T(4,128)S(1)} %get-tuple-element.40), channel_id=1, source_target_pairs={{0,1},{1,0},{2,3},{3,2},{4,5},{5,4},{6,7},{7,6},{8,9},{9,8},{10,11... | collective-permute-start | bytes 442376 | tf_op jit(solution)/shard_map/ppermute | solution.py:288
  85.1 6.1 %shard_map.66 = (f32[1,18,4,512]{3,2,1,0:T(4,128)S(1)}, f32[1,18,4,512]{3,2,1,0:T(4,128)S(1)}) custom-call(s32[128]{0:T(128)S(1)} %compare_select_fusion.4.place, bf16[4,672,128]{2,1,0:T(8,128)(2,1)S(1)} %pad_maximum_fusion.own, bf16[4,672,128]{2,1,0:T(8,128)(2,1)S(1)} %collective-permute-done.14.other, f32[18,36,8,128]{3,2,1,0:T(8,128)} %copy-done, ...), custom_call_target="tpu_custom_call" | custom-call | flops 4320000000 | bytes 1000000 | tf_op jit(solution)/shard_map/pallas_call | solution.py:195
  91.2 3.1 %collective-permute-done.18.p3 = f32[18,4,512]{2,1,0:T(4,128)S(1)} collective-permute-done((f32[18,4,512]{2,1,0:T(4,128)S(1)}, f32[18,4,512]{2,1,0:T(4,128)S(1)}, u32[]{:S(2)}, u32[]{:S(2)}) %collective-permute-start.18) | collective-permute-done | bytes 147488 | tf_op jit(solution)/shard_map/ppermute | solution.py:288
  94.3 5.1 %collective-permute-done.16.p1 = f32[18,4,512]{2,1,0:T(4,128)S(1)} collective-permute-done((f32[18,4,512]{2,1,0:T(4,128)S(1)}, f32[18,4,512]{2,1,0:T(4,128)S(1)}, u32[]{:S(2)}, u32[]{:S(2)}) %collective-permute-start.16) | collective-permute-done | bytes 147488 | tf_op jit(solution)/shard_map/ppermute | solution.py:288
  99.4 0.5 collective-permute-start.19
  99.9 1.0 collective-permute-done.19.t0
  100.9 1.0 shard_map.67
  (35 shorter events, 1.3 us)
Async XLA Ops:
  5.6 4.5 %copy-start.3 = (s32[2]{0:T(128)S(1)}, s32[2]{0:T(128)}, u32[]{:S(2)}) copy-start(s32[2]{0:T(128)} %param.8) | copy-start | bytes 28
  6.8 6.2 %collective-permute-start = (bf16[2,4,672,128]{3,2,0,1:T(8,128)(2,1)}, bf16[2,4,672,128]{3,2,0,1:T(8,128)(2,1)S(1)}, u32[]{:S(2)}, u32[]{:S(2)}) collective-permute-start(bf16[2,4,672,128]{3,2,0,1:T(8,128)(2,1)} %fusion.2), channel_id=1, source_target_pairs={{0,4},{4,0},{8,12},{12,8},{16,20},{20,16},{24,28},{28,24},{32,36},... | collective-permute-start | bytes 4128776 | tf_op jit(solution)/shard_map/ppermute | solution.py:48
  13.4 3.4 %copy-start.2 = (f32[2,18,2,128]{3,2,1,0:T(2,128)S(1)}, f32[2,18,2,128]{3,2,1,0:T(2,128)}, u32[]{:S(2)}) copy-start(f32[2,18,2,128]{3,2,1,0:T(2,128)} %constant.35.clone) | copy-start | bytes 110596
  13.5 11.4 %collective-permute-start.3 = (bf16[2,672,128]{2,1,0:T(8,128)(2,1)S(1)}, bf16[2,672,128]{2,1,0:T(8,128)(2,1)S(1)}, u32[]{:S(2)}, u32[]{:S(2)}) collective-permute-start(bf16[2,672,128]{2,1,0:T(8,128)(2,1)S(1)} %get-tuple-element.35), channel_id=1, source_target_pairs={{0,192},{4,28},{8,200},{12,20},{16,208},{20,12},{24,216},{28,4},{3... | collective-permute-start | bytes 1032200 | tf_op jit(solution)/shard_map/ppermute | solution.py:48
  14.6 10.3 %collective-permute-start.2 = (bf16[2,672,128]{2,1,0:T(8,128)(2,1)S(1)}, bf16[2,672,128]{2,1,0:T(8,128)(2,1)S(1)}, u32[]{:S(2)}, u32[]{:S(2)}) collective-permute-start(bf16[2,672,128]{2,1,0:T(8,128)(2,1)S(1)} %get-tuple-element.36), channel_id=1, source_target_pairs={{0,128},{4,20},{8,136},{12,28},{16,144},{20,4},{24,152},{28,12},{3... | collective-permute-start | bytes 1032200 | tf_op jit(solution)/shard_map/ppermute | solution.py:48
  14.9 10.6 %collective-permute-start.1 = (bf16[2,672,128]{2,1,0:T(8,128)(2,1)S(1)}, bf16[2,672,128]{2,1,0:T(8,128)(2,1)S(1)}, u32[]{:S(2)}, u32[]{:S(2)}) collective-permute-start(bf16[2,672,128]{2,1,0:T(8,128)(2,1)S(1)} %get-tuple-element.37), channel_id=1, source_target_pairs={{0,64},{4,12},{8,72},{12,4},{16,80},{20,28},{24,88},{28,20},{32,96... | collective-permute-start | bytes 1032200 | tf_op jit(solution)/shard_map/ppermute | solution.py:48
  25.6 5.2 %collective-permute-start.6 = (bf16[2,168,128]{2,1,0:T(8,128)(2,1)S(1)}, bf16[2,168,128]{2,1,0:T(8,128)(2,1)S(1)}, u32[]{:S(2)}, u32[]{:S(2)}) collective-permute-start(bf16[2,168,128]{2,1,0:T(8,128)(2,1)S(1)} %get-tuple-element.49), channel_id=1, source_target_pairs={{0,24},{4,196},{8,16},{12,204},{16,8},{20,212},{24,0},{28,220},{32... | collective-permute-start | bytes 258056 | tf_op jit(solution)/shard_map/ppermute | solution.py:48
  26.6 4.8 %collective-permute-start.5 = (bf16[2,168,128]{2,1,0:T(8,128)(2,1)S(1)}, bf16[2,168,128]{2,1,0:T(8,128)(2,1)S(1)}, u32[]{:S(2)}, u32[]{:S(2)}) collective-permute-start(bf16[2,168,128]{2,1,0:T(8,128)(2,1)S(1)} %get-tuple-element.50), channel_id=1, source_target_pairs={{0,16},{4,132},{8,24},{12,140},{16,0},{20,148},{24,8},{28,156},{32... | collective-permute-start | bytes 258056 | tf_op jit(solution)/shard_map/ppermute | solution.py:48
  27.1 4.9 %collective-permute-start.4 = (bf16[2,168,128]{2,1,0:T(8,128)(2,1)S(1)}, bf16[2,168,128]{2,1,0:T(8,128)(2,1)S(1)}, u32[]{:S(2)}, u32[]{:S(2)}) collective-permute-start(bf16[2,168,128]{2,1,0:T(8,128)(2,1)S(1)} %get-tuple-element.51), channel_id=1, source_target_pairs={{0,8},{4,68},{8,0},{12,76},{16,24},{20,84},{24,16},{28,92},{32,40}... | collective-permute-start | bytes 258056 | tf_op jit(solution)/shard_map/ppermute | solution.py:48
  30.9 20.4 %copy-start = (f32[18,36,8,128]{3,2,1,0:T(8,128)}, f32[18,36,8,128]{3,2,1,0:T(8,128)S(1)}, u32[]{:S(2)}) copy-start(f32[18,36,8,128]{3,2,1,0:T(8,128)S(1)} %shard_map.64.right) | copy-start | bytes 7962628
  32.1 3.4 %collective-permute-start.7 = (bf16[2,168,128]{2,1,0:T(8,128)(2,1)S(1)}, bf16[2,168,128]{2,1,0:T(8,128)(2,1)S(1)}, u32[]{:S(2)}, u32[]{:S(2)}) collective-permute-start(bf16[2,168,128]{2,1,0:T(8,128)(2,1)S(1)} %slice_select_fusion.2), channel_id=1, source_target_pairs={{0,32},{4,36},{8,40},{12,44},{16,48},{20,52},{24,56},{28,60},{32,0... | collective-permute-start | bytes 258056 | tf_op jit(solution)/shard_map/ppermute | solution.py:48
  35.5 4.6 %collective-permute-start.10 = (bf16[2,168,128]{2,1,0:T(8,128)(2,1)S(1)}, bf16[2,168,128]{2,1,0:T(8,128)(2,1)S(1)}, u32[]{:S(2)}, u32[]{:S(2)}) collective-permute-start(bf16[2,168,128]{2,1,0:T(8,128)(2,1)S(1)} %broadcast_select_fusion.9), channel_id=1, source_target_pairs={{0,24},{4,196},{8,16},{12,204},{16,8},{20,212},{24,0},{28,220},{32... | collective-permute-start | bytes 258056 | tf_op jit(solution)/shard_map/ppermute | solution.py:48
  36.8 4.8 %collective-permute-start.9 = (bf16[2,168,128]{2,1,0:T(8,128)(2,1)S(1)}, bf16[2,168,128]{2,1,0:T(8,128)(2,1)S(1)}, u32[]{:S(2)}, u32[]{:S(2)}) collective-permute-start(bf16[2,168,128]{2,1,0:T(8,128)(2,1)S(1)} %broadcast_select_fusion.9), channel_id=1, source_target_pairs={{0,16},{4,132},{8,24},{12,140},{16,0},{20,148},{24,8},{28,156},{32... | collective-permute-start | bytes 258056 | tf_op jit(solution)/shard_map/ppermute | solution.py:48
  37.7 4.0 %collective-permute-start.8 = (bf16[2,168,128]{2,1,0:T(8,128)(2,1)S(1)}, bf16[2,168,128]{2,1,0:T(8,128)(2,1)S(1)}, u32[]{:S(2)}, u32[]{:S(2)}) collective-permute-start(bf16[2,168,128]{2,1,0:T(8,128)(2,1)S(1)} %broadcast_select_fusion.9), channel_id=1, source_target_pairs={{0,8},{4,68},{8,0},{12,76},{16,24},{20,84},{24,16},{28,92},{32,40}... | collective-permute-start | bytes 258056 | tf_op jit(solution)/shard_map/ppermute | solution.py:48
  41.7 9.5 %collective-permute-start.12 = (bf16[2,672,128]{2,1,0:T(8,128)(2,1)S(1)}, bf16[2,672,128]{2,1,0:T(8,128)(2,1)S(1)}, u32[]{:S(2)}, u32[]{:S(2)}) collective-permute-start(bf16[2,672,128]{2,1,0:T(8,128)(2,1)S(1)} %pad_maximum_fusion.2), channel_id=1, source_target_pairs={{0,128},{4,20},{8,136},{12,28},{16,144},{20,4},{24,152},{28,12},{3... | collective-permute-start | bytes 1032200 | tf_op jit(solution)/shard_map/ppermute | solution.py:48
  44.4 9.7 %collective-permute-start.11 = (bf16[2,672,128]{2,1,0:T(8,128)(2,1)S(1)}, bf16[2,672,128]{2,1,0:T(8,128)(2,1)S(1)}, u32[]{:S(2)}, u32[]{:S(2)}) collective-permute-start(bf16[2,672,128]{2,1,0:T(8,128)(2,1)S(1)} %pad_maximum_fusion.2), channel_id=1, source_target_pairs={{0,64},{4,12},{8,72},{12,4},{16,80},{20,28},{24,88},{28,20},{32,96... | collective-permute-start | bytes 1032200 | tf_op jit(solution)/shard_map/ppermute | solution.py:48
  44.8 10.0 %collective-permute-start.13 = (bf16[2,672,128]{2,1,0:T(8,128)(2,1)S(1)}, bf16[2,672,128]{2,1,0:T(8,128)(2,1)S(1)}, u32[]{:S(2)}, u32[]{:S(2)}) collective-permute-start(bf16[2,672,128]{2,1,0:T(8,128)(2,1)S(1)} %pad_maximum_fusion.2), channel_id=1, source_target_pairs={{0,192},{4,28},{8,200},{12,20},{16,208},{20,12},{24,216},{28,4},{3... | collective-permute-start | bytes 1032200 | tf_op jit(solution)/shard_map/ppermute | solution.py:48
  55.0 7.9 %collective-permute-start.14 = (bf16[4,672,128]{2,1,0:T(8,128)(2,1)S(1)}, bf16[4,672,128]{2,1,0:T(8,128)(2,1)S(1)}, u32[]{:S(2)}, u32[]{:S(2)}) collective-permute-start(bf16[4,672,128]{2,1,0:T(8,128)(2,1)S(1)} %pad_maximum_fusion.1), channel_id=1, source_target_pairs={{0,4},{4,0},{8,12},{12,8},{16,20},{20,16},{24,28},{28,24},{32,36},... | collective-permute-start | bytes 2064392 | tf_op jit(solution)/shard_map/ppermute | solution.py:48
  74.6 1.9 %collective-permute-start.15 = (f32[3,18,4,512]{3,2,1,0:T(4,128)S(1)}, f32[3,18,4,512]{3,2,1,0:T(4,128)S(1)}, u32[]{:S(2)}, u32[]{:S(2)}) collective-permute-start(f32[3,18,4,512]{3,2,1,0:T(4,128)S(1)} %get-tuple-element.20), channel_id=1, source_target_pairs={{0,4},{4,0},{8,12},{12,8},{16,20},{20,16},{24,28},{28,24},{32,36},... | collective-permute-start | bytes 1327112 | tf_op jit(solution)/shard_map/ppermute | solution.py:48
  76.7 17.6 %collective-permute-start.18 = (f32[18,4,512]{2,1,0:T(4,128)S(1)}, f32[18,4,512]{2,1,0:T(4,128)S(1)}, u32[]{:S(2)}, u32[]{:S(2)}) collective-permute-start(f32[18,4,512]{2,1,0:T(4,128)S(1)} %get-tuple-element.38), channel_id=1, source_target_pairs={{0,3},{1,2},{2,1},{3,0},{4,7},{5,6},{6,5},{7,4},{8,11},{9,10},{10,... | collective-permute-start | bytes 442376 | tf_op jit(solution)/shard_map/ppermute | solution.py:288
  82.9 11.4 %collective-permute-start.17 = (f32[18,4,512]{2,1,0:T(4,128)S(1)}, f32[18,4,512]{2,1,0:T(4,128)S(1)}, u32[]{:S(2)}, u32[]{:S(2)}) collective-permute-start(f32[18,4,512]{2,1,0:T(4,128)S(1)} %get-tuple-element.39), channel_id=1, source_target_pairs={{0,2},{1,3},{2,0},{3,1},{4,6},{5,7},{6,4},{7,5},{8,10},{9,11},{10,... | collective-permute-start | bytes 442376 | tf_op jit(solution)/shard_map/ppermute | solution.py:288
  83.9 17.0 %copy-start.1 = (f32[256,256]{1,0:T(8,128)S(1)}, f32[256,256]{1,0:T(8,128)}, u32[]{:S(2)}) copy-start(f32[256,256]{1,0:T(8,128)} %constant.37.clone.flip) | copy-start | bytes 786436
  83.9 15.5 %collective-permute-start.16 = (f32[18,4,512]{2,1,0:T(4,128)S(1)}, f32[18,4,512]{2,1,0:T(4,128)S(1)}, u32[]{:S(2)}, u32[]{:S(2)}) collective-permute-start(f32[18,4,512]{2,1,0:T(4,128)S(1)} %get-tuple-element.40), channel_id=1, source_target_pairs={{0,1},{1,0},{2,3},{3,2},{4,5},{5,4},{6,7},{7,6},{8,9},{9,8},{10,11... | collective-permute-start | bytes 442376 | tf_op jit(solution)/shard_map/ppermute | solution.py:288
  99.4 1.5 %collective-permute-start.19 = (f32[1,18,4,512]{3,2,1,0:T(4,128)S(1)}, f32[1,18,4,512]{3,2,1,0:T(4,128)S(1)}, u32[]{:S(2)}, u32[]{:S(2)}) collective-permute-start(f32[1,18,4,512]{3,2,1,0:T(4,128)S(1)} %get-tuple-element.25), channel_id=1, source_target_pairs={{0,4},{4,0},{8,12},{12,8},{16,20},{20,16},{24,28},{28,24},{32,36},... | collective-permute-start | bytes 442376 | tf_op jit(solution)/shard_map/ppermute | solution.py:48

commit v3 on v2

--- a/solution.py
+++ b/solution.py
@@ -54,6 +54,11 @@
 
 def along_second(value, distance):
     return pair_permute(value, distance << 1, distance << 4)
+
+
+def swap_window(value, distance):
+    size = lax.axis_size("window")
+    return lax.ppermute(value, "window", [(w, w ^ distance) for w in range(size)])
 
 
 def pick(which, values):
@@ -211,10 +216,10 @@
     )(place, own, other, right, basis)
 
 
-def finish_kernel(m0, t0, p1, p2, p3, flip, out):
-    total = (m0[0] + t0[0]) + (p1[...] + (p2[...] + p3[...]))
-    even = total[:, :, 0:HALF]
-    odd = total[:, :, HALF:LAGS]
+def finish_kernel(m0, t0, left, left_end, late, late_end, flip, out):
+    total = m0[0] + t0[0]
+    even = total[:, :, 0:HALF] + (left[0] + left_end[...])
+    odd = total[:, :, HALF:LAGS] + (late[0] + late_end[...])
     early = jnp.dot((even + odd).reshape(72, HALF), flip[...], precision=lax.Precision.HIGHEST,
                     preferred_element_type=jnp.float32)
     out[0, :, :, :, :, 0:HALF] = early.reshape(STEPS, 3, 3, 4, HALF)
@@ -272,10 +277,10 @@
                         jnp.broadcast_to(core, (LANES,)), near[1][1], near[1][0]])
     block = jnp.where(root_core == core, whole, across)
     parts = [block[:, 0]] + [along_first(block[:, d], d) for d in range(1, WAYS)]
-    piece = pick(first, parts)
+    piece, right = lax.optimization_barrier((pick(first, parts), right))
     cuts = [piece[:, d * sub:(d + 1) * sub] for d in range(WAYS)]
     parts = [cuts[0]] + [along_second(cuts[d], d) for d in range(1, WAYS)]
-    small, right = lax.optimization_barrier((pick(second, parts), right))
+    small = pick(second, parts)
     small = jnp.where(root_z == z, small, pair_permute(small, 8))
     piece = jnp.concatenate([small] + [along_second(small, d) for d in range(1, WAYS)], 1)
     pieces = [piece] + [along_first(piece, d) for d in range(1, WAYS)]
@@ -285,12 +290,15 @@
     kept, given = correlate((1, 2, 3), place, own, other, right, basis)
     total = kept + pair_permute(given, 1)
     place, total = lax.optimization_barrier((place, total))
-    parts = [lax.ppermute(total[d - 1], "window", [(w, w ^ d) for w in range(windows)])
-             for d in range(1, windows)]
+    left = swap_window(jnp.stack([total[0], total[1]])[..., :HALF], 1)
+    late = swap_window(jnp.stack([total[2], total[1]])[..., HALF:], 3)
     kept, given = correlate((0,), place, own, other, right, basis)
-    given, parts = lax.optimization_barrier((given, parts))
+    given, left, late = lax.optimization_barrier((given, left, late))
+    given = pair_permute(given, 1)
+    left_end = swap_window(total[2][..., :HALF] + left[1], 3)
+    late_end = swap_window(total[0][..., HALF:] + late[1], 1)
     flip = jnp.asarray(np.eye(HALF, dtype=np.float32)[::-1].copy())
-    return finish([kept, pair_permute(given, 1)] + parts, flip).transpose(0, 1, 2, 4, 3, 5)
+    return finish([kept, given, left, left_end, late, late_end], flip).transpose(0, 1, 2, 4, 3, 5)
 
 
 def solution(mesh):

time: 102 us -> 102 us (level)
  waiting for transfers between devices: 38.1 us -> 35.5 us
  starting transfers between devices: 33.6 us -> 35.9 us
    ppermute x3 -> x4, starting transfers between devices: 8.47 us -> 10.1 us  [swap_window(): lax.ppermute(value, 'window', [(w, w ^ distance) for w in range(size)])]
    ppermute x3 -> x4, waiting for transfers between devices: 8.19 us -> 6.52 us  [swap_window(): lax.ppermute(value, 'window', [(w, w ^ distance) for w in range(size)])]
  transfers between devices with their start and end apart: 20 -> 21, of which waited for: 16 -> 17; matrix products, arithmetic and copies ran while one was open for 2% -> 2% of each run, Pallas kernels for 8% -> 8%
where the time goes in v3:
time: 102 us
  starting transfers between devices  35.9 us (35%)
  waiting for transfers between devices  35.5 us (35%)
  Pallas kernels  20.5 us (20%)
  other arithmetic  6.9 us (7%)
  local copies, waits for them, and re-layouts  2.66 us (3%)
    ppermute x17, waiting for transfers between devices, pair_permute(): lax.ppermute(value, 'station', [(s, s ^ shifts[s & 1]) for s in range(siz...  29 us
    ppermute x17, starting transfers between devices, pair_permute(): lax.ppermute(value, 'station', [(s, s ^ shifts[s & 1]) for s in range(siz...  25.8 us
    pallas_call x2, Pallas kernels, correlate(): pl.pallas_call(functools.partial(correlate_kernel, slots), in_specs=[pl.B...  17.8 us
    ppermute x4, starting transfers between devices, swap_window(): lax.ppermute(value, 'window', [(w, w ^ distance) for w in range(size)])  10.1 us
    ppermute x4, waiting for transfers between devices, swap_window(): lax.ppermute(value, 'window', [(w, w ^ distance) for w in range(size)])  6.52 us
    mul x1, other arithmetic, body(): masked = spectra * valid_mask.astype(jnp.bfloat16)[:, :, None, None, None]  2.52 us
  transfers between devices with their start and end apart: 21, of which 17 were waited for; matrix products, arithmetic and copies ran while one was open for 2% of the time, Pallas kernels for 8%

profile of v3, /device:TPU:1, one launch (start us, length us, event | category | flops | bytes accessed | tf_op | source)
XLA Modules:
  0.0 101.7 jit_solution(18380898166893950338)
XLA Ops:
  0.0 0.7 convert_element_type.5
  0.7 2.5 %broadcast_multiply_fusion = bf16[4,6,3,2,4608]{4,3,2,1,0:T(2,128)(2,1)S(1)} fusion(bf16[4,6,3,2,4608]{4,3,2,1,0:T(2,128)(2,1)} %param.6, bf16[4,6]{1,0:T(4,128)(2,1)S(1)} %convert_element_type.5), kind=kLoop, calls=%fused_computation.11 | loop fusion | flops 663552 | bytes 2654256 | tf_op jit(solution)/shard_map/mul | solution.py:255
  3.2 0.9 reshape.45
  4.1 0.4 fusion.6
  4.6 0.5 copy.8
  5.1 0.5 copy.9
  5.6 1.2 %fusion.2 = bf16[2,4,672,128]{3,2,0,1:T(8,128)(2,1)} fusion(bf16[1,4,648,128]{3,2,0,1:T(8,128)(2,1)S(1)} %bitcast.51, bf16[1,4,648,128]{3,2,0,1:T(8,128)(2,1)S(1)} %bitcast.49), kind=kLoop, calls=%fused_computation.3 | loop fusion | flops 4816896 | bytes 2703360 | tf_op jit(solution)/shard_map/stack | solution.py:259
  6.9 3.2 %collective-permute-start = (bf16[2,4,672,128]{3,2,0,1:T(8,128)(2,1)}, bf16[2,4,672,128]{3,2,0,1:T(8,128)(2,1)S(1)}, u32[]{:S(2)}, u32[]{:S(2)}) collective-permute-start(bf16[2,4,672,128]{3,2,0,1:T(8,128)(2,1)} %fusion.2), channel_id=1, source_target_pairs={{0,4},{4,0},{8,12},{12,8},{16,20},{20,16},{24,28},{28,24},{32,36},... | collective-permute-start | bytes 4128776 | tf_op jit(solution)/shard_map/ppermute | solution.py:48
  10.2 1.4 %fusion.4.own = bf16[4,672,128]{2,1,0:T(8,128)(2,1)S(1)} fusion(bf16[2,4,672,128]{3,2,0,1:T(8,128)(2,1)} %fusion.2, pred[]{:T(512)S(6)} %eq.69), kind=kLoop, calls=%fused_computation.8 | loop fusion | flops 344064 | bytes 2064385 | tf_op jit(solution)/shard_map/jit(_where)/select_n | solution.py:261
  11.6 1.5 %collective-permute-done = bf16[2,4,672,128]{3,2,0,1:T(8,128)(2,1)S(1)} collective-permute-done((bf16[2,4,672,128]{3,2,0,1:T(8,128)(2,1)}, bf16[2,4,672,128]{3,2,0,1:T(8,128)(2,1)S(1)}, u32[]{:S(2)}, u32[]{:S(2)}) %collective-permute-start) | collective-permute-done | bytes 1376288 | tf_op jit(solution)/shard_map/ppermute | solution.py:48
  13.5 1.1 %collective-permute-start.3 = (bf16[2,672,128]{2,1,0:T(8,128)(2,1)S(1)}, bf16[2,672,128]{2,1,0:T(8,128)(2,1)S(1)}, u32[]{:S(2)}, u32[]{:S(2)}) collective-permute-start(bf16[2,672,128]{2,1,0:T(8,128)(2,1)S(1)} %get-tuple-element.33), channel_id=1, source_target_pairs={{0,192},{4,28},{8,200},{12,20},{16,208},{20,12},{24,216},{28,4},{3... | collective-permute-start | bytes 1032200 | tf_op jit(solution)/shard_map/ppermute | solution.py:48
  15.0 1.9 %collective-permute-start.1 = (bf16[2,672,128]{2,1,0:T(8,128)(2,1)S(1)}, bf16[2,672,128]{2,1,0:T(8,128)(2,1)S(1)}, u32[]{:S(2)}, u32[]{:S(2)}) collective-permute-start(bf16[2,672,128]{2,1,0:T(8,128)(2,1)S(1)} %get-tuple-element.35), channel_id=1, source_target_pairs={{0,64},{4,12},{8,72},{12,4},{16,80},{20,28},{24,88},{28,20},{32,96... | collective-permute-start | bytes 1032200 | tf_op jit(solution)/shard_map/ppermute | solution.py:48
  16.9 1.8 %shard_map.64.right = f32[18,36,8,128]{3,2,1,0:T(8,128)S(1)} custom-call(bf16[4,672,128]{2,1,0:T(8,128)(2,1)S(1)} %fusion.4.own, bf16[4,672,128]{2,1,0:T(8,128)(2,1)S(1)} %fusion.3.other, f32[18,2,128]{2,1,0:T(2,128)S(1)} %dynamic-slice_bitcast_fusion.turns), custom_call_target="tpu_custom_call" | custom-call | flops 10000000 | bytes 1000000 | tf_op jit(solution)/shard_map/pallas_call | solution.py:97
  18.7 6.1 %collective-permute-done.3 = bf16[2,672,128]{2,1,0:T(8,128)(2,1)S(1)} collective-permute-done((bf16[2,672,128]{2,1,0:T(8,128)(2,1)S(1)}, bf16[2,672,128]{2,1,0:T(8,128)(2,1)S(1)}, u32[]{:S(2)}, u32[]{:S(2)}) %collective-permute-start.3) | collective-permute-done | bytes 344096 | tf_op jit(solution)/shard_map/ppermute | solution.py:48
  24.9 0.6 collective-permute-done.1
  25.6 1.0 collective-permute-start.6
  26.6 0.5 collective-permute-start.5
  27.1 1.8 %collective-permute-start.4 = (bf16[2,168,128]{2,1,0:T(8,128)(2,1)S(1)}, bf16[2,168,128]{2,1,0:T(8,128)(2,1)S(1)}, u32[]{:S(2)}, u32[]{:S(2)}) collective-permute-start(bf16[2,168,128]{2,1,0:T(8,128)(2,1)S(1)} %get-tuple-element.50), channel_id=1, source_target_pairs={{0,8},{4,68},{8,0},{12,76},{16,24},{20,84},{24,16},{28,92},{32,40}... | collective-permute-start | bytes 258056 | tf_op jit(solution)/shard_map/ppermute | solution.py:48
  29.0 1.3 %collective-permute-done.6 = bf16[2,168,128]{2,1,0:T(8,128)(2,1)S(1)} collective-permute-done((bf16[2,168,128]{2,1,0:T(8,128)(2,1)S(1)}, bf16[2,168,128]{2,1,0:T(8,128)(2,1)S(1)}, u32[]{:S(2)}, u32[]{:S(2)}) %collective-permute-start.6) | collective-permute-done | bytes 86048 | tf_op jit(solution)/shard_map/ppermute | solution.py:48
  30.2 1.2 %collective-permute-done.5 = bf16[2,168,128]{2,1,0:T(8,128)(2,1)S(1)} collective-permute-done((bf16[2,168,128]{2,1,0:T(8,128)(2,1)S(1)}, bf16[2,168,128]{2,1,0:T(8,128)(2,1)S(1)}, u32[]{:S(2)}, u32[]{:S(2)}) %collective-permute-start.5) | collective-permute-done | bytes 86048 | tf_op jit(solution)/shard_map/ppermute | solution.py:48
  31.4 0.6 collective-permute-done.4
  32.1 1.1 %collective-permute-start.7 = (bf16[2,168,128]{2,1,0:T(8,128)(2,1)S(1)}, bf16[2,168,128]{2,1,0:T(8,128)(2,1)S(1)}, u32[]{:S(2)}, u32[]{:S(2)}) collective-permute-start(bf16[2,168,128]{2,1,0:T(8,128)(2,1)S(1)} %select_select_fusion), channel_id=1, source_target_pairs={{0,32},{4,36},{8,40},{12,44},{16,48},{20,52},{24,56},{28,60},{32,0... | collective-permute-start | bytes 258056 | tf_op jit(solution)/shard_map/ppermute | solution.py:48
  33.2 2.3 %collective-permute-done.7 = bf16[2,168,128]{2,1,0:T(8,128)(2,1)S(1)} collective-permute-done((bf16[2,168,128]{2,1,0:T(8,128)(2,1)S(1)}, bf16[2,168,128]{2,1,0:T(8,128)(2,1)S(1)}, u32[]{:S(2)}, u32[]{:S(2)}) %collective-permute-start.7) | collective-permute-done | bytes 86048 | tf_op jit(solution)/shard_map/ppermute | solution.py:48
  35.5 1.3 %collective-permute-start.10 = (bf16[2,168,128]{2,1,0:T(8,128)(2,1)S(1)}, bf16[2,168,128]{2,1,0:T(8,128)(2,1)S(1)}, u32[]{:S(2)}, u32[]{:S(2)}) collective-permute-start(bf16[2,168,128]{2,1,0:T(8,128)(2,1)S(1)} %broadcast_select_fusion.9), channel_id=1, source_target_pairs={{0,24},{4,196},{8,16},{12,204},{16,8},{20,212},{24,0},{28,220},{32... | collective-permute-start | bytes 258056 | tf_op jit(solution)/shard_map/ppermute | solution.py:48
  36.8 0.9 collective-permute-start.9
  37.6 1.2 %collective-permute-start.8 = (bf16[2,168,128]{2,1,0:T(8,128)(2,1)S(1)}, bf16[2,168,128]{2,1,0:T(8,128)(2,1)S(1)}, u32[]{:S(2)}, u32[]{:S(2)}) collective-permute-start(bf16[2,168,128]{2,1,0:T(8,128)(2,1)S(1)} %broadcast_select_fusion.9), channel_id=1, source_target_pairs={{0,8},{4,68},{8,0},{12,76},{16,24},{20,84},{24,16},{28,92},{32,40}... | collective-permute-start | bytes 258056 | tf_op jit(solution)/shard_map/ppermute | solution.py:48
  38.9 1.3 %collective-permute-done.10 = bf16[2,168,128]{2,1,0:T(8,128)(2,1)S(1)} collective-permute-done((bf16[2,168,128]{2,1,0:T(8,128)(2,1)S(1)}, bf16[2,168,128]{2,1,0:T(8,128)(2,1)S(1)}, u32[]{:S(2)}, u32[]{:S(2)}) %collective-permute-start.10) | collective-permute-done | bytes 86048 | tf_op jit(solution)/shard_map/ppermute | solution.py:48
  40.2 1.5 %collective-permute-done.9 = bf16[2,168,128]{2,1,0:T(8,128)(2,1)S(1)} collective-permute-done((bf16[2,168,128]{2,1,0:T(8,128)(2,1)S(1)}, bf16[2,168,128]{2,1,0:T(8,128)(2,1)S(1)}, u32[]{:S(2)}, u32[]{:S(2)}) %collective-permute-start.9) | collective-permute-done | bytes 86048 | tf_op jit(solution)/shard_map/ppermute | solution.py:48
  41.7 2.7 %collective-permute-start.12 = (bf16[2,672,128]{2,1,0:T(8,128)(2,1)S(1)}, bf16[2,672,128]{2,1,0:T(8,128)(2,1)S(1)}, u32[]{:S(2)}, u32[]{:S(2)}) collective-permute-start(bf16[2,672,128]{2,1,0:T(8,128)(2,1)S(1)} %pad_maximum_fusion.2), channel_id=1, source_target_pairs={{0,128},{4,20},{8,136},{12,28},{16,144},{20,4},{24,152},{28,12},{3... | collective-permute-start | bytes 1032200 | tf_op jit(solution)/shard_map/ppermute | solution.py:48
  44.4 0.4 collective-permute-start.11
  44.8 0.5 collective-permute-start.13
  45.3 5.8 %collective-permute-done.12 = bf16[2,672,128]{2,1,0:T(8,128)(2,1)S(1)} collective-permute-done((bf16[2,672,128]{2,1,0:T(8,128)(2,1)S(1)}, bf16[2,672,128]{2,1,0:T(8,128)(2,1)S(1)}, u32[]{:S(2)}, u32[]{:S(2)}) %collective-permute-start.12) | collective-permute-done | bytes 344096 | tf_op jit(solution)/shard_map/ppermute | solution.py:48
  51.2 2.9 %collective-permute-done.11 = bf16[2,672,128]{2,1,0:T(8,128)(2,1)S(1)} collective-permute-done((bf16[2,672,128]{2,1,0:T(8,128)(2,1)S(1)}, bf16[2,672,128]{2,1,0:T(8,128)(2,1)S(1)}, u32[]{:S(2)}, u32[]{:S(2)}) %collective-permute-start.11) | collective-permute-done | bytes 344096 | tf_op jit(solution)/shard_map/ppermute | solution.py:48
  54.1 0.8 collective-permute-done.13
  55.0 6.1 %collective-permute-start.14 = (bf16[4,672,128]{2,1,0:T(8,128)(2,1)S(1)}, bf16[4,672,128]{2,1,0:T(8,128)(2,1)S(1)}, u32[]{:S(2)}, u32[]{:S(2)}) collective-permute-start(bf16[4,672,128]{2,1,0:T(8,128)(2,1)S(1)} %pad_maximum_fusion.1), channel_id=1, source_target_pairs={{0,4},{4,0},{8,12},{12,8},{16,20},{20,16},{24,28},{28,24},{32,36},... | collective-permute-start | bytes 2064392 | tf_op jit(solution)/shard_map/ppermute | solution.py:48
  61.2 1.7 %collective-permute-done.14.other = bf16[4,672,128]{2,1,0:T(8,128)(2,1)S(1)} collective-permute-done((bf16[4,672,128]{2,1,0:T(8,128)(2,1)S(1)}, bf16[4,672,128]{2,1,0:T(8,128)(2,1)S(1)}, u32[]{:S(2)}, u32[]{:S(2)}) %collective-permute-start.14) | collective-permute-done | bytes 688160 | tf_op jit(solution)/shard_map/ppermute | solution.py:48
  62.9 11.7 %shard_map.65 = (f32[3,18,4,512]{3,2,1,0:T(4,128)S(1)}, f32[3,18,4,512]{3,2,1,0:T(4,128)S(1)}) custom-call(s32[128]{0:T(128)S(1)} %compare_select_fusion.4.place, bf16[4,672,128]{2,1,0:T(8,128)(2,1)S(1)} %pad_maximum_fusion.own, bf16[4,672,128]{2,1,0:T(8,128)(2,1)S(1)} %collective-permute-done.14.other, f32[18,36,8,128]{3,2,1,0:T(8,128)} %copy-done, ...), custom_call_target="tpu_custom_call" | custom-call | flops 12960000000 | bytes 1000000 | tf_op jit(solution)/shard_map/pallas_call | solution.py:200
  74.6 0.5 collective-permute-start.15
  75.1 1.4 %collective-permute-done.15 = f32[3,18,4,512]{3,2,1,0:T(4,128)S(1)} collective-permute-done((f32[3,18,4,512]{3,2,1,0:T(4,128)S(1)}, f32[3,18,4,512]{3,2,1,0:T(4,128)S(1)}, u32[]{:S(2)}, u32[]{:S(2)}) %collective-permute-start.15) | collective-permute-done | bytes 442400 | tf_op jit(solution)/shard_map/ppermute | solution.py:48
  76.7 6.3 %collective-permute-start.17 = (f32[2,18,4,256]{3,2,1,0:T(4,128)S(1)}, f32[2,18,4,256]{3,2,1,0:T(4,128)S(1)}, u32[]{:S(2)}, u32[]{:S(2)}) collective-permute-start(f32[2,18,4,256]{3,2,1,0:T(4,128)S(1)} %pad_maximum_fusion.3), channel_id=1, source_target_pairs={{0,3},{1,2},{2,1},{3,0},{4,7},{5,6},{6,5},{7,4},{8,11},{9,10},{10,... | collective-permute-start | bytes 442376 | tf_op jit(solution)/shard_map/ppermute | solution.py:61
  83.0 1.2 %collective-permute-start.16 = (f32[2,18,4,256]{3,2,1,0:T(4,128)S(1)}, f32[2,18,4,256]{3,2,1,0:T(4,128)S(1)}, u32[]{:S(2)}, u32[]{:S(2)}) collective-permute-start(f32[2,18,4,256]{3,2,1,0:T(4,128)S(1)} %slice.138), channel_id=1, source_target_pairs={{0,1},{1,0},{2,3},{3,2},{4,5},{5,4},{6,7},{7,6},{8,9},{9,8},{10,11... | collective-permute-start | bytes 442376 | tf_op jit(solution)/shard_map/ppermute | solution.py:61
  84.2 6.1 %shard_map.66 = (f32[1,18,4,512]{3,2,1,0:T(4,128)S(1)}, f32[1,18,4,512]{3,2,1,0:T(4,128)S(1)}) custom-call(s32[128]{0:T(128)S(1)} %compare_select_fusion.4.place, bf16[4,672,128]{2,1,0:T(8,128)(2,1)S(1)} %pad_maximum_fusion.own, bf16[4,672,128]{2,1,0:T(8,128)(2,1)S(1)} %collective-permute-done.14.other, f32[18,36,8,128]{3,2,1,0:T(8,128)} %copy-done, ...), custom_call_target="tpu_custom_call" | custom-call | flops 4320000000 | bytes 1000000 | tf_op jit(solution)/shard_map/pallas_call | solution.py:200
  90.3 0.9 collective-permute-done.16.left
  91.2 2.5 %collective-permute-start.19 = (f32[18,4,256]{2,1,0:T(4,128)S(1)}, f32[18,4,256]{2,1,0:T(4,128)S(1)}, u32[]{:S(2)}, u32[]{:S(2)}) collective-permute-start(f32[18,4,256]{2,1,0:T(4,128)S(1)} %slice_add_fusion.1), channel_id=1, source_target_pairs={{0,3},{1,2},{2,1},{3,0},{4,7},{5,6},{6,5},{7,4},{8,11},{9,10},{10,... | collective-permute-start | bytes 221192 | tf_op jit(solution)/shard_map/ppermute | solution.py:61
  93.8 1.2 %collective-permute-start.18 = (f32[1,18,4,512]{3,2,1,0:T(4,128)S(1)}, f32[1,18,4,512]{3,2,1,0:T(4,128)S(1)}, u32[]{:S(2)}, u32[]{:S(2)}) collective-permute-start(f32[1,18,4,512]{3,2,1,0:T(4,128)S(1)} %get-tuple-element.24), channel_id=1, source_target_pairs={{0,4},{4,0},{8,12},{12,8},{16,20},{20,16},{24,28},{28,24},{32,36},... | collective-permute-start | bytes 442376 | tf_op jit(solution)/shard_map/ppermute | solution.py:48
  95.1 1.6 %collective-permute-done.19.left_end = f32[18,4,256]{2,1,0:T(4,128)S(1)} collective-permute-done((f32[18,4,256]{2,1,0:T(4,128)S(1)}, f32[18,4,256]{2,1,0:T(4,128)S(1)}, u32[]{:S(2)}, u32[]{:S(2)}) %collective-permute-start.19) | collective-permute-done | bytes 73760 | tf_op jit(solution)/shard_map/ppermute | solution.py:61
  96.7 4.1 %collective-permute-done.20.late_end = f32[18,4,256]{2,1,0:T(4,128)S(1)} collective-permute-done((f32[18,4,256]{2,1,0:T(4,128)S(1)}, f32[18,4,256]{2,1,0:T(4,128)S(1)}, u32[]{:S(2)}, u32[]{:S(2)}) %collective-permute-start.20) | collective-permute-done | bytes 73760 | tf_op jit(solution)/shard_map/ppermute | solution.py:61
  100.8 1.0 shard_map.67
  (41 shorter events, 1.9 us)
Async XLA Ops:
  5.6 4.5 %copy-start.3 = (s32[2]{0:T(128)S(1)}, s32[2]{0:T(128)}, u32[]{:S(2)}) copy-start(s32[2]{0:T(128)} %param.8) | copy-start | bytes 28
  6.9 6.2 %collective-permute-start = (bf16[2,4,672,128]{3,2,0,1:T(8,128)(2,1)}, bf16[2,4,672,128]{3,2,0,1:T(8,128)(2,1)S(1)}, u32[]{:S(2)}, u32[]{:S(2)}) collective-permute-start(bf16[2,4,672,128]{3,2,0,1:T(8,128)(2,1)} %fusion.2), channel_id=1, source_target_pairs={{0,4},{4,0},{8,12},{12,8},{16,20},{20,16},{24,28},{28,24},{32,36},... | collective-permute-start | bytes 4128776 | tf_op jit(solution)/shard_map/ppermute | solution.py:48
  13.4 3.4 %copy-start.2 = (f32[2,18,2,128]{3,2,1,0:T(2,128)S(1)}, f32[2,18,2,128]{3,2,1,0:T(2,128)}, u32[]{:S(2)}) copy-start(f32[2,18,2,128]{3,2,1,0:T(2,128)} %constant.35.clone) | copy-start | bytes 110596
  13.5 11.4 %collective-permute-start.3 = (bf16[2,672,128]{2,1,0:T(8,128)(2,1)S(1)}, bf16[2,672,128]{2,1,0:T(8,128)(2,1)S(1)}, u32[]{:S(2)}, u32[]{:S(2)}) collective-permute-start(bf16[2,672,128]{2,1,0:T(8,128)(2,1)S(1)} %get-tuple-element.33), channel_id=1, source_target_pairs={{0,192},{4,28},{8,200},{12,20},{16,208},{20,12},{24,216},{28,4},{3... | collective-permute-start | bytes 1032200 | tf_op jit(solution)/shard_map/ppermute | solution.py:48
  14.6 10.3 %collective-permute-start.2 = (bf16[2,672,128]{2,1,0:T(8,128)(2,1)S(1)}, bf16[2,672,128]{2,1,0:T(8,128)(2,1)S(1)}, u32[]{:S(2)}, u32[]{:S(2)}) collective-permute-start(bf16[2,672,128]{2,1,0:T(8,128)(2,1)S(1)} %get-tuple-element.34), channel_id=1, source_target_pairs={{0,128},{4,20},{8,136},{12,28},{16,144},{20,4},{24,152},{28,12},{3... | collective-permute-start | bytes 1032200 | tf_op jit(solution)/shard_map/ppermute | solution.py:48
  15.0 10.6 %collective-permute-start.1 = (bf16[2,672,128]{2,1,0:T(8,128)(2,1)S(1)}, bf16[2,672,128]{2,1,0:T(8,128)(2,1)S(1)}, u32[]{:S(2)}, u32[]{:S(2)}) collective-permute-start(bf16[2,672,128]{2,1,0:T(8,128)(2,1)S(1)} %get-tuple-element.35), channel_id=1, source_target_pairs={{0,64},{4,12},{8,72},{12,4},{16,80},{20,28},{24,88},{28,20},{32,96... | collective-permute-start | bytes 1032200 | tf_op jit(solution)/shard_map/ppermute | solution.py:48
  18.7 16.8 %copy-start = (f32[18,36,8,128]{3,2,1,0:T(8,128)}, f32[18,36,8,128]{3,2,1,0:T(8,128)S(1)}, u32[]{:S(2)}) copy-start(f32[18,36,8,128]{3,2,1,0:T(8,128)S(1)} %shard_map.64.right) | copy-start | bytes 7962628
  25.6 4.6 %collective-permute-start.6 = (bf16[2,168,128]{2,1,0:T(8,128)(2,1)S(1)}, bf16[2,168,128]{2,1,0:T(8,128)(2,1)S(1)}, u32[]{:S(2)}, u32[]{:S(2)}) collective-permute-start(bf16[2,168,128]{2,1,0:T(8,128)(2,1)S(1)} %get-tuple-element.48), channel_id=1, source_target_pairs={{0,24},{4,196},{8,16},{12,204},{16,8},{20,212},{24,0},{28,220},{32... | collective-permute-start | bytes 258056 | tf_op jit(solution)/shard_map/ppermute | solution.py:48
  26.6 4.8 %collective-permute-start.5 = (bf16[2,168,128]{2,1,0:T(8,128)(2,1)S(1)}, bf16[2,168,128]{2,1,0:T(8,128)(2,1)S(1)}, u32[]{:S(2)}, u32[]{:S(2)}) collective-permute-start(bf16[2,168,128]{2,1,0:T(8,128)(2,1)S(1)} %get-tuple-element.49), channel_id=1, source_target_pairs={{0,16},{4,132},{8,24},{12,140},{16,0},{20,148},{24,8},{28,156},{32... | collective-permute-start | bytes 258056 | tf_op jit(solution)/shard_map/ppermute | solution.py:48
  27.1 4.9 %collective-permute-start.4 = (bf16[2,168,128]{2,1,0:T(8,128)(2,1)S(1)}, bf16[2,168,128]{2,1,0:T(8,128)(2,1)S(1)}, u32[]{:S(2)}, u32[]{:S(2)}) collective-permute-start(bf16[2,168,128]{2,1,0:T(8,128)(2,1)S(1)} %get-tuple-element.50), channel_id=1, source_target_pairs={{0,8},{4,68},{8,0},{12,76},{16,24},{20,84},{24,16},{28,92},{32,40}... | collective-permute-start | bytes 258056 | tf_op jit(solution)/shard_map/ppermute | solution.py:48
  32.1 3.4 %collective-permute-start.7 = (bf16[2,168,128]{2,1,0:T(8,128)(2,1)S(1)}, bf16[2,168,128]{2,1,0:T(8,128)(2,1)S(1)}, u32[]{:S(2)}, u32[]{:S(2)}) collective-permute-start(bf16[2,168,128]{2,1,0:T(8,128)(2,1)S(1)} %select_select_fusion), channel_id=1, source_target_pairs={{0,32},{4,36},{8,40},{12,44},{16,48},{20,52},{24,56},{28,60},{32,0... | collective-permute-start | bytes 258056 | tf_op jit(solution)/shard_map/ppermute | solution.py:48
  35.5 4.6 %collective-permute-start.10 = (bf16[2,168,128]{2,1,0:T(8,128)(2,1)S(1)}, bf16[2,168,128]{2,1,0:T(8,128)(2,1)S(1)}, u32[]{:S(2)}, u32[]{:S(2)}) collective-permute-start(bf16[2,168,128]{2,1,0:T(8,128)(2,1)S(1)} %broadcast_select_fusion.9), channel_id=1, source_target_pairs={{0,24},{4,196},{8,16},{12,204},{16,8},{20,212},{24,0},{28,220},{32... | collective-permute-start | bytes 258056 | tf_op jit(solution)/shard_map/ppermute | solution.py:48
  36.8 4.8 %collective-permute-start.9 = (bf16[2,168,128]{2,1,0:T(8,128)(2,1)S(1)}, bf16[2,168,128]{2,1,0:T(8,128)(2,1)S(1)}, u32[]{:S(2)}, u32[]{:S(2)}) collective-permute-start(bf16[2,168,128]{2,1,0:T(8,128)(2,1)S(1)} %broadcast_select_fusion.9), channel_id=1, source_target_pairs={{0,16},{4,132},{8,24},{12,140},{16,0},{20,148},{24,8},{28,156},{32... | collective-permute-start | bytes 258056 | tf_op jit(solution)/shard_map/ppermute | solution.py:48
  37.6 4.0 %collective-permute-start.8 = (bf16[2,168,128]{2,1,0:T(8,128)(2,1)S(1)}, bf16[2,168,128]{2,1,0:T(8,128)(2,1)S(1)}, u32[]{:S(2)}, u32[]{:S(2)}) collective-permute-start(bf16[2,168,128]{2,1,0:T(8,128)(2,1)S(1)} %broadcast_select_fusion.9), channel_id=1, source_target_pairs={{0,8},{4,68},{8,0},{12,76},{16,24},{20,84},{24,16},{28,92},{32,40}... | collective-permute-start | bytes 258056 | tf_op jit(solution)/shard_map/ppermute | solution.py:48
  41.7 9.5 %collective-permute-start.12 = (bf16[2,672,128]{2,1,0:T(8,128)(2,1)S(1)}, bf16[2,672,128]{2,1,0:T(8,128)(2,1)S(1)}, u32[]{:S(2)}, u32[]{:S(2)}) collective-permute-start(bf16[2,672,128]{2,1,0:T(8,128)(2,1)S(1)} %pad_maximum_fusion.2), channel_id=1, source_target_pairs={{0,128},{4,20},{8,136},{12,28},{16,144},{20,4},{24,152},{28,12},{3... | collective-permute-start | bytes 1032200 | tf_op jit(solution)/shard_map/ppermute | solution.py:48
  44.4 9.7 %collective-permute-start.11 = (bf16[2,672,128]{2,1,0:T(8,128)(2,1)S(1)}, bf16[2,672,128]{2,1,0:T(8,128)(2,1)S(1)}, u32[]{:S(2)}, u32[]{:S(2)}) collective-permute-start(bf16[2,672,128]{2,1,0:T(8,128)(2,1)S(1)} %pad_maximum_fusion.2), channel_id=1, source_target_pairs={{0,64},{4,12},{8,72},{12,4},{16,80},{20,28},{24,88},{28,20},{32,96... | collective-permute-start | bytes 1032200 | tf_op jit(solution)/shard_map/ppermute | solution.py:48
  44.8 10.0 %collective-permute-start.13 = (bf16[2,672,128]{2,1,0:T(8,128)(2,1)S(1)}, bf16[2,672,128]{2,1,0:T(8,128)(2,1)S(1)}, u32[]{:S(2)}, u32[]{:S(2)}) collective-permute-start(bf16[2,672,128]{2,1,0:T(8,128)(2,1)S(1)} %pad_maximum_fusion.2), channel_id=1, source_target_pairs={{0,192},{4,28},{8,200},{12,20},{16,208},{20,12},{24,216},{28,4},{3... | collective-permute-start | bytes 1032200 | tf_op jit(solution)/shard_map/ppermute | solution.py:48
  55.0 7.9 %collective-permute-start.14 = (bf16[4,672,128]{2,1,0:T(8,128)(2,1)S(1)}, bf16[4,672,128]{2,1,0:T(8,128)(2,1)S(1)}, u32[]{:S(2)}, u32[]{:S(2)}) collective-permute-start(bf16[4,672,128]{2,1,0:T(8,128)(2,1)S(1)} %pad_maximum_fusion.1), channel_id=1, source_target_pairs={{0,4},{4,0},{8,12},{12,8},{16,20},{20,16},{24,28},{28,24},{32,36},... | collective-permute-start | bytes 2064392 | tf_op jit(solution)/shard_map/ppermute | solution.py:48
  74.6 1.9 %collective-permute-start.15 = (f32[3,18,4,512]{3,2,1,0:T(4,128)S(1)}, f32[3,18,4,512]{3,2,1,0:T(4,128)S(1)}, u32[]{:S(2)}, u32[]{:S(2)}) collective-permute-start(f32[3,18,4,512]{3,2,1,0:T(4,128)S(1)} %get-tuple-element.19), channel_id=1, source_target_pairs={{0,4},{4,0},{8,12},{12,8},{16,20},{20,16},{24,28},{28,24},{32,36},... | collective-permute-start | bytes 1327112 | tf_op jit(solution)/shard_map/ppermute | solution.py:48
  76.7 24.0 %copy-start.1 = (f32[256,256]{1,0:T(8,128)S(1)}, f32[256,256]{1,0:T(8,128)}, u32[]{:S(2)}) copy-start(f32[256,256]{1,0:T(8,128)} %constant.37.clone.flip) | copy-start | bytes 786436
  76.7 13.5 %collective-permute-start.17 = (f32[2,18,4,256]{3,2,1,0:T(4,128)S(1)}, f32[2,18,4,256]{3,2,1,0:T(4,128)S(1)}, u32[]{:S(2)}, u32[]{:S(2)}) collective-permute-start(f32[2,18,4,256]{3,2,1,0:T(4,128)S(1)} %pad_maximum_fusion.3), channel_id=1, source_target_pairs={{0,3},{1,2},{2,1},{3,0},{4,7},{5,6},{6,5},{7,4},{8,11},{9,10},{10,... | collective-permute-start | bytes 442376 | tf_op jit(solution)/shard_map/ppermute | solution.py:61
  83.0 8.2 %collective-permute-start.16 = (f32[2,18,4,256]{3,2,1,0:T(4,128)S(1)}, f32[2,18,4,256]{3,2,1,0:T(4,128)S(1)}, u32[]{:S(2)}, u32[]{:S(2)}) collective-permute-start(f32[2,18,4,256]{3,2,1,0:T(4,128)S(1)} %slice.138), channel_id=1, source_target_pairs={{0,1},{1,0},{2,3},{3,2},{4,5},{5,4},{6,7},{7,6},{8,9},{9,8},{10,11... | collective-permute-start | bytes 442376 | tf_op jit(solution)/shard_map/ppermute | solution.py:61
  91.2 5.5 %collective-permute-start.19 = (f32[18,4,256]{2,1,0:T(4,128)S(1)}, f32[18,4,256]{2,1,0:T(4,128)S(1)}, u32[]{:S(2)}, u32[]{:S(2)}) collective-permute-start(f32[18,4,256]{2,1,0:T(4,128)S(1)} %slice_add_fusion.1), channel_id=1, source_target_pairs={{0,3},{1,2},{2,1},{3,0},{4,7},{5,6},{6,5},{7,4},{8,11},{9,10},{10,... | collective-permute-start | bytes 221192 | tf_op jit(solution)/shard_map/ppermute | solution.py:61
  93.8 7.0 %collective-permute-start.18 = (f32[1,18,4,512]{3,2,1,0:T(4,128)S(1)}, f32[1,18,4,512]{3,2,1,0:T(4,128)S(1)}, u32[]{:S(2)}, u32[]{:S(2)}) collective-permute-start(f32[1,18,4,512]{3,2,1,0:T(4,128)S(1)} %get-tuple-element.24), channel_id=1, source_target_pairs={{0,4},{4,0},{8,12},{12,8},{16,20},{20,16},{24,28},{28,24},{32,36},... | collective-permute-start | bytes 442376 | tf_op jit(solution)/shard_map/ppermute | solution.py:48
  95.0 5.8 %collective-permute-start.20 = (f32[18,4,256]{2,1,0:T(4,128)S(1)}, f32[18,4,256]{2,1,0:T(4,128)S(1)}, u32[]{:S(2)}, u32[]{:S(2)}) collective-permute-start(f32[18,4,256]{2,1,0:T(4,128)S(1)} %slice_add_fusion), channel_id=1, source_target_pairs={{0,1},{1,0},{2,3},{3,2},{4,5},{5,4},{6,7},{7,6},{8,9},{9,8},{10,11... | collective-permute-start | bytes 221192 | tf_op jit(solution)/shard_map/ppermute | solution.py:61

commit v4 on v3

--- a/solution.py
+++ b/solution.py
@@ -165,10 +165,10 @@
     acc[...] = jnp.zeros_like(acc)
     for step, pieces in ((core, own), (1 - core, other)):
         first, second = place[4 * step], place[4 * step + 1]
-        for near in range(WAYS):
-            piece = pieces[near].astype(jnp.float32)
+        for used in slots:
+            piece = pieces[first ^ window ^ used].astype(jnp.float32)
             for number in range(WAYS):
-                at = pl.multiple_of(step * size + (first ^ near) * rows + (second ^ number) * sub, 8)
+                at = pl.multiple_of(step * size + (window ^ used) * rows + (second ^ number) * sub, 8)
                 owner[pl.ds(at, sub), :] = piece[number * sub:(number + 1) * sub]
     cross(0, 0)
 
@@ -256,12 +256,11 @@
     masked = masked.reshape(stations, hours * comps, 2, tiles, LANES).transpose(0, 1, 3, 2, 4)
     halves = [masked[:, :, n * half:(n + 1) * half].reshape(stations, used, LANES)
               for n in range(CORES)]
-    whole = pad_rows(jnp.stack(halves), rows)
-    across = pair_permute(whole, 1)
-    own = jnp.where(core == 0, whole[0], whole[1])
-    other = jnp.where(core == 0, across[0], across[1])
+    rest = pad_rows(jnp.stack([h[1:] for h in halves]), rows)
+    lead = pad_rows(jnp.stack([h[0] for h in halves]), rows)
+    far_rest = pair_permute(rest, 1)
+    own = pad_rows(jnp.where(core == 0, halves[0], halves[1]), rows)
     turns = lax.dynamic_index_in_dim(jnp.asarray(turns), core, 0, keepdims=False)
-    right = turn_right(own, other, turns)
 
     roots = lax.optimization_barrier(jnp.broadcast_to(plan[:, None], (STEPS, LANES)))
     lane = lax.iota(jnp.int32, LANES)
@@ -275,8 +274,13 @@
     _, root_z, _, root_core = coords(mine)
     place = pick(lane, [near[0][0], near[0][1], jnp.broadcast_to(window, (LANES,)),
                         jnp.broadcast_to(core, (LANES,)), near[1][1], near[1][0]])
-    block = jnp.where(root_core == core, whole, across)
-    parts = [block[:, 0]] + [along_first(block[:, d], d) for d in range(1, WAYS)]
+    block = jnp.where(root_core == core, rest, far_rest)
+    parts = [along_first(block[:, d - 1], d) for d in range(1, WAYS)]
+    far_lead = pair_permute(lead, 1)
+    parts = [jnp.where(root_core == core, lead, far_lead)] + parts
+    other = jnp.concatenate([jnp.where(core == 0, far_lead[0], far_lead[1])[None],
+                             jnp.where(core == 0, far_rest[0], far_rest[1])], 0)
+    right = turn_right(own, other, turns)
     piece, right = lax.optimization_barrier((pick(first, parts), right))
     cuts = [piece[:, d * sub:(d + 1) * sub] for d in range(WAYS)]
     parts = [cuts[0]] + [along_second(cuts[d], d) for d in range(1, WAYS)]

time: 102 us -> 105 us (1.029)
  other arithmetic: 6.9 us -> 9.44 us
  local copies, waits for them, and re-layouts: 2.66 us -> 4.37 us
    select_n x0 -> x1, local copies, waits for them, and re-layouts: none -> 1.7 us  [body(): own = pad_rows(jnp.where(core == 0, halves[0], halves[1]), rows)]
    ppermute x17 -> x18, waiting for transfers between devices: 29 us -> 27.5 us  [pair_permute(): lax.ppermute(value, 'station', [(s, s ^ shifts[s & 1]) for s in range(siz...]
    select_n x3, other arithmetic: 0.1 us -> 1.24 us  [pick(): result = jnp.where(which == number, values[number], result)]
    select_n x3 -> x4, other arithmetic: 1.81 us -> 2.51 us  [the longest x1 1.15 us: body(): own = pad_rows(jnp.where(core == 0, halves[0], halves[1]), rows)]
    ppermute x17 -> x18, starting transfers between devices: 25.8 us -> 25.8 us  [pair_permute(): lax.ppermute(value, 'station', [(s, s ^ shifts[s & 1]) for s in range(siz...]
  transfers between devices with their start and end apart: 21 -> 22, of which waited for: 17 -> 16; matrix products, arithmetic and copies ran while one was open for 2% -> 6% of each run, Pallas kernels for 8% -> 7%
where the time goes in v4:
time: 105 us
  starting transfers between devices  36 us (34%)
  waiting for transfers between devices  34.6 us (33%)
  Pallas kernels  20.5 us (20%)
  other arithmetic  9.44 us (9%)
  local copies, waits for them, and re-layouts  4.37 us (4%)
    ppermute x18, waiting for transfers between devices, pair_permute(): lax.ppermute(value, 'station', [(s, s ^ shifts[s & 1]) for s in range(siz...  27.5 us
    ppermute x18, starting transfers between devices, pair_permute(): lax.ppermute(value, 'station', [(s, s ^ shifts[s & 1]) for s in range(siz...  25.8 us
    pallas_call x2, Pallas kernels, correlate(): pl.pallas_call(functools.partial(correlate_kernel, slots), in_specs=[pl.B...  17.8 us
    ppermute x4, starting transfers between devices, swap_window(): lax.ppermute(value, 'window', [(w, w ^ distance) for w in range(size)])  10.1 us
    ppermute x4, waiting for transfers between devices, swap_window(): lax.ppermute(value, 'window', [(w, w ^ distance) for w in range(size)])  7.02 us
    mul x1, other arithmetic, body(): masked = spectra * valid_mask.astype(jnp.bfloat16)[:, :, None, None, None]  2.52 us
  transfers between devices with their start and end apart: 22, of which 16 were waited for; matrix products, arithmetic and copies ran while one was open for 6% of the time, Pallas kernels for 7%

profile of v4, /device:TPU:1, one launch (start us, length us, event | category | flops | bytes accessed | tf_op | source)
XLA Modules:
  0.0 105.2 jit_solution(9040725517299921973)
XLA Ops:
  0.0 0.7 convert_element_type.9
  0.7 2.5 %broadcast_multiply_fusion = bf16[4,6,3,2,4608]{4,3,2,1,0:T(2,128)(2,1)S(1)} fusion(bf16[4,6,3,2,4608]{4,3,2,1,0:T(2,128)(2,1)} %param.6, bf16[4,6]{1,0:T(4,128)(2,1)S(1)} %convert_element_type.9), kind=kLoop, calls=%fused_computation.12 | loop fusion | flops 663552 | bytes 2654256 | tf_op jit(solution)/shard_map/mul | solution.py:255
  3.2 0.9 reshape.53
  4.5 0.8 fusion.6
  5.3 3.2 %collective-permute-start = (bf16[2,672,128]{2,1,0:T(8,128)(2,1)}, bf16[2,672,128]{2,1,0:T(8,128)(2,1)}, u32[]{:S(2)}, u32[]{:S(2)}) collective-permute-start(bf16[2,672,128]{2,1,0:T(8,128)(2,1)} %fusion.6), channel_id=1, source_target_pairs={{0,4},{4,0},{8,12},{12,8},{16,20},{20,16},{24,28},{28,24},{32,36},... | collective-permute-start | bytes 1032200 | tf_op jit(solution)/shard_map/ppermute | solution.py:48
  8.9 0.4 copy.10
  9.7 1.1 %fusion.2 = bf16[2,3,672,128]{3,2,0,1:T(8,128)(2,1)} fusion(bf16[1,3,648,128]{3,2,0,1:T(8,128)(2,1)S(1)} %bitcast.50, bf16[1,3,648,128]{3,2,0,1:T(8,128)(2,1)S(1)} %bitcast.48), kind=kLoop, calls=%fused_computation.3 | loop fusion | flops 3612672 | bytes 2027520 | tf_op jit(solution)/shard_map/stack | solution.py:259
  10.7 1.1 %slice_select_fusion = bf16[4,18,18,2,128]{4,2,3,1,0:T(8,128)(2,1)} fusion(bf16[4,18,36,2,128]{4,2,3,1,0:T(8,128)(2,1)S(1)} %bitcast.47, pred[]{:T(512)S(6)} %eq.72), kind=kLoop, calls=%fused_computation.5 | loop fusion | flops 331776 | bytes 1990657 | tf_op jit(solution)/shard_map/jit(_where)/select_n | solution.py:262
  12.0 1.7 %copy.12 = bf16[4,18,18,2,128]{4,3,2,1,0:T(2,128)(2,1)S(1)} copy(bf16[4,18,18,2,128]{4,2,3,1,0:T(8,128)(2,1)} %slice_select_fusion) | data formatting | bytes 1327104 | tf_op jit(solution)/shard_map/jit(_where)/select_n | solution.py:262
  13.8 1.0 slice_select_fusion.2
  15.2 1.1 %collective-permute-start.4 = (bf16[2,672,128]{2,1,0:T(8,128)(2,1)S(1)}, bf16[2,672,128]{2,1,0:T(8,128)(2,1)S(1)}, u32[]{:S(2)}, u32[]{:S(2)}) collective-permute-start(bf16[2,672,128]{2,1,0:T(8,128)(2,1)S(1)} %get-tuple-element.35), channel_id=1, source_target_pairs={{0,192},{4,28},{8,200},{12,20},{16,208},{20,12},{24,216},{28,4},{3... | collective-permute-start | bytes 1032200 | tf_op jit(solution)/shard_map/ppermute | solution.py:48
  16.7 1.9 %collective-permute-start.2 = (bf16[2,672,128]{2,1,0:T(8,128)(2,1)S(1)}, bf16[2,672,128]{2,1,0:T(8,128)(2,1)S(1)}, u32[]{:S(2)}, u32[]{:S(2)}) collective-permute-start(bf16[2,672,128]{2,1,0:T(8,128)(2,1)S(1)} %get-tuple-element.37), channel_id=1, source_target_pairs={{0,64},{4,12},{8,72},{12,4},{16,80},{20,28},{24,88},{28,20},{32,96... | collective-permute-start | bytes 1032200 | tf_op jit(solution)/shard_map/ppermute | solution.py:48
  18.7 1.8 %shard_map.64.right = f32[18,36,8,128]{3,2,1,0:T(8,128)S(1)} custom-call(bf16[4,672,128]{2,1,0:T(8,128)(2,1)S(1)} %pad.14.own, bf16[4,672,128]{2,1,0:T(8,128)(2,1)S(1)} %pad_maximum_fusion.other, f32[18,2,128]{2,1,0:T(2,128)S(1)} %dynamic-slice_bitcast_fusion.turns), custom_call_target="tpu_custom_call" | custom-call | flops 10000000 | bytes 1000000 | tf_op jit(solution)/shard_map/pallas_call | solution.py:97
  20.5 6.1 %collective-permute-done.4 = bf16[2,672,128]{2,1,0:T(8,128)(2,1)S(1)} collective-permute-done((bf16[2,672,128]{2,1,0:T(8,128)(2,1)S(1)}, bf16[2,672,128]{2,1,0:T(8,128)(2,1)S(1)}, u32[]{:S(2)}, u32[]{:S(2)}) %collective-permute-start.4) | collective-permute-done | bytes 344096 | tf_op jit(solution)/shard_map/ppermute | solution.py:48
  26.6 0.6 collective-permute-done.2
  27.2 1.2 %select_select_fusion = bf16[2,672,128]{2,1,0:T(8,128)(2,1)S(1)} fusion(bf16[2,672,128]{2,1,0:T(8,128)(2,1)S(1)} %collective-permute-done.2, bf16[2,672,128]{2,1,0:T(8,128)(2,1)S(1)} %collective-permute-done.3, bf16[2,672,128]{2,1,0:T(8,128)(2,1)S(1)} %collective-permute-done.4, bf16[2,672,128]{2,1,0:T(8,128)(2,1)} %collective-permute-done, ...), kind=kLoop, calls=%fused_computation.20 | loop fusion | flops 1892352 | bytes 2052608 | tf_op jit(solution)/shard_map/jit(_where)/select_n | solution.py:67
  28.5 1.0 collective-permute-start.7
  29.5 0.5 collective-permute-start.6
  30.0 1.8 %collective-permute-start.5 = (bf16[2,168,128]{2,1,0:T(8,128)(2,1)S(1)}, bf16[2,168,128]{2,1,0:T(8,128)(2,1)S(1)}, u32[]{:S(2)}, u32[]{:S(2)}) collective-permute-start(bf16[2,168,128]{2,1,0:T(8,128)(2,1)S(1)} %get-tuple-element.52), channel_id=1, source_target_pairs={{0,8},{4,68},{8,0},{12,76},{16,24},{20,84},{24,16},{28,92},{32,40}... | collective-permute-start | bytes 258056 | tf_op jit(solution)/shard_map/ppermute | solution.py:48
  31.8 1.3 %collective-permute-done.7 = bf16[2,168,128]{2,1,0:T(8,128)(2,1)S(1)} collective-permute-done((bf16[2,168,128]{2,1,0:T(8,128)(2,1)S(1)}, bf16[2,168,128]{2,1,0:T(8,128)(2,1)S(1)}, u32[]{:S(2)}, u32[]{:S(2)}) %collective-permute-start.7) | collective-permute-done | bytes 86048 | tf_op jit(solution)/shard_map/ppermute | solution.py:48
  33.1 1.2 %collective-permute-done.6 = bf16[2,168,128]{2,1,0:T(8,128)(2,1)S(1)} collective-permute-done((bf16[2,168,128]{2,1,0:T(8,128)(2,1)S(1)}, bf16[2,168,128]{2,1,0:T(8,128)(2,1)S(1)}, u32[]{:S(2)}, u32[]{:S(2)}) %collective-permute-start.6) | collective-permute-done | bytes 86048 | tf_op jit(solution)/shard_map/ppermute | solution.py:48
  34.3 0.6 collective-permute-done.5
  34.9 1.1 %collective-permute-start.8 = (bf16[2,168,128]{2,1,0:T(8,128)(2,1)S(1)}, bf16[2,168,128]{2,1,0:T(8,128)(2,1)S(1)}, u32[]{:S(2)}, u32[]{:S(2)}) collective-permute-start(bf16[2,168,128]{2,1,0:T(8,128)(2,1)S(1)} %select_select_fusion.1), channel_id=1, source_target_pairs={{0,32},{4,36},{8,40},{12,44},{16,48},{20,52},{24,56},{28,60},{32,0... | collective-permute-start | bytes 258056 | tf_op jit(solution)/shard_map/ppermute | solution.py:48
  36.0 2.3 %collective-permute-done.8 = bf16[2,168,128]{2,1,0:T(8,128)(2,1)S(1)} collective-permute-done((bf16[2,168,128]{2,1,0:T(8,128)(2,1)S(1)}, bf16[2,168,128]{2,1,0:T(8,128)(2,1)S(1)}, u32[]{:S(2)}, u32[]{:S(2)}) %collective-permute-start.8) | collective-permute-done | bytes 86048 | tf_op jit(solution)/shard_map/ppermute | solution.py:48
  38.4 1.3 %collective-permute-start.11 = (bf16[2,168,128]{2,1,0:T(8,128)(2,1)S(1)}, bf16[2,168,128]{2,1,0:T(8,128)(2,1)S(1)}, u32[]{:S(2)}, u32[]{:S(2)}) collective-permute-start(bf16[2,168,128]{2,1,0:T(8,128)(2,1)S(1)} %broadcast_select_fusion.9), channel_id=1, source_target_pairs={{0,24},{4,196},{8,16},{12,204},{16,8},{20,212},{24,0},{28,220},{32... | collective-permute-start | bytes 258056 | tf_op jit(solution)/shard_map/ppermute | solution.py:48
  39.6 0.8 collective-permute-start.10
  40.5 1.2 %collective-permute-start.9 = (bf16[2,168,128]{2,1,0:T(8,128)(2,1)S(1)}, bf16[2,168,128]{2,1,0:T(8,128)(2,1)S(1)}, u32[]{:S(2)}, u32[]{:S(2)}) collective-permute-start(bf16[2,168,128]{2,1,0:T(8,128)(2,1)S(1)} %broadcast_select_fusion.9), channel_id=1, source_target_pairs={{0,8},{4,68},{8,0},{12,76},{16,24},{20,84},{24,16},{28,92},{32,40}... | collective-permute-start | bytes 258056 | tf_op jit(solution)/shard_map/ppermute | solution.py:48
  41.7 1.3 %collective-permute-done.11 = bf16[2,168,128]{2,1,0:T(8,128)(2,1)S(1)} collective-permute-done((bf16[2,168,128]{2,1,0:T(8,128)(2,1)S(1)}, bf16[2,168,128]{2,1,0:T(8,128)(2,1)S(1)}, u32[]{:S(2)}, u32[]{:S(2)}) %collective-permute-start.11) | collective-permute-done | bytes 86048 | tf_op jit(solution)/shard_map/ppermute | solution.py:48
  43.0 1.5 %collective-permute-done.10 = bf16[2,168,128]{2,1,0:T(8,128)(2,1)S(1)} collective-permute-done((bf16[2,168,128]{2,1,0:T(8,128)(2,1)S(1)}, bf16[2,168,128]{2,1,0:T(8,128)(2,1)S(1)}, u32[]{:S(2)}, u32[]{:S(2)}) %collective-permute-start.10) | collective-permute-done | bytes 86048 | tf_op jit(solution)/shard_map/ppermute | solution.py:48
  44.5 2.7 %collective-permute-start.13 = (bf16[2,672,128]{2,1,0:T(8,128)(2,1)S(1)}, bf16[2,672,128]{2,1,0:T(8,128)(2,1)S(1)}, u32[]{:S(2)}, u32[]{:S(2)}) collective-permute-start(bf16[2,672,128]{2,1,0:T(8,128)(2,1)S(1)} %pad_maximum_fusion.3), channel_id=1, source_target_pairs={{0,128},{4,20},{8,136},{12,28},{16,144},{20,4},{24,152},{28,12},{3... | collective-permute-start | bytes 1032200 | tf_op jit(solution)/shard_map/ppermute | solution.py:48
  47.2 0.4 collective-permute-start.12
  48.0 6.2 %collective-permute-done.13 = bf16[2,672,128]{2,1,0:T(8,128)(2,1)S(1)} collective-permute-done((bf16[2,672,128]{2,1,0:T(8,128)(2,1)S(1)}, bf16[2,672,128]{2,1,0:T(8,128)(2,1)S(1)}, u32[]{:S(2)}, u32[]{:S(2)}) %collective-permute-start.13) | collective-permute-done | bytes 344096 | tf_op jit(solution)/shard_map/ppermute | solution.py:48
  54.2 2.9 %collective-permute-done.12 = bf16[2,672,128]{2,1,0:T(8,128)(2,1)S(1)} collective-permute-done((bf16[2,672,128]{2,1,0:T(8,128)(2,1)S(1)}, bf16[2,672,128]{2,1,0:T(8,128)(2,1)S(1)}, u32[]{:S(2)}, u32[]{:S(2)}) %collective-permute-start.12) | collective-permute-done | bytes 344096 | tf_op jit(solution)/shard_map/ppermute | solution.py:48
  57.1 0.5 collective-permute-done.14
  57.8 6.4 %collective-permute-start.15 = (bf16[4,672,128]{2,1,0:T(8,128)(2,1)S(1)}, bf16[4,672,128]{2,1,0:T(8,128)(2,1)S(1)}, u32[]{:S(2)}, u32[]{:S(2)}) collective-permute-start(bf16[4,672,128]{2,1,0:T(8,128)(2,1)S(1)} %pad_maximum_fusion.2), channel_id=1, source_target_pairs={{0,4},{4,0},{8,12},{12,8},{16,20},{20,16},{24,28},{28,24},{32,36},... | collective-permute-start | bytes 2064392 | tf_op jit(solution)/shard_map/ppermute | solution.py:48
  64.2 1.7 %collective-permute-done.15.other = bf16[4,672,128]{2,1,0:T(8,128)(2,1)S(1)} collective-permute-done((bf16[4,672,128]{2,1,0:T(8,128)(2,1)S(1)}, bf16[4,672,128]{2,1,0:T(8,128)(2,1)S(1)}, u32[]{:S(2)}, u32[]{:S(2)}) %collective-permute-start.15) | collective-permute-done | bytes 688160 | tf_op jit(solution)/shard_map/ppermute | solution.py:48
  65.9 11.7 %shard_map.65 = (f32[3,18,4,512]{3,2,1,0:T(4,128)S(1)}, f32[3,18,4,512]{3,2,1,0:T(4,128)S(1)}) custom-call(s32[128]{0:T(128)S(1)} %compare_select_fusion.4.place, bf16[4,672,128]{2,1,0:T(8,128)(2,1)S(1)} %pad_maximum_fusion.1.own, bf16[4,672,128]{2,1,0:T(8,128)(2,1)S(1)} %collective-permute-done.15.other, f32[18,36,8,128]{3,2,1,0:T(8,128)} %copy-done, ...), custom_call_target="tpu_custom_call" | custom-call | flops 12960000000 | bytes 1000000 | tf_op jit(solution)/shard_map/pallas_call | solution.py:200
  77.6 0.5 collective-permute-start.16
  78.0 1.4 %collective-permute-done.16 = f32[3,18,4,512]{3,2,1,0:T(4,128)S(1)} collective-permute-done((f32[3,18,4,512]{3,2,1,0:T(4,128)S(1)}, f32[3,18,4,512]{3,2,1,0:T(4,128)S(1)}, u32[]{:S(2)}, u32[]{:S(2)}) %collective-permute-start.16) | collective-permute-done | bytes 442400 | tf_op jit(solution)/shard_map/ppermute | solution.py:48
  79.7 6.3 %collective-permute-start.18 = (f32[2,18,4,256]{3,2,1,0:T(4,128)S(1)}, f32[2,18,4,256]{3,2,1,0:T(4,128)S(1)}, u32[]{:S(2)}, u32[]{:S(2)}) collective-permute-start(f32[2,18,4,256]{3,2,1,0:T(4,128)S(1)} %pad_maximum_fusion.4), channel_id=1, source_target_pairs={{0,3},{1,2},{2,1},{3,0},{4,7},{5,6},{6,5},{7,4},{8,11},{9,10},{10,... | collective-permute-start | bytes 442376 | tf_op jit(solution)/shard_map/ppermute | solution.py:61
  86.0 1.2 %collective-permute-start.17 = (f32[2,18,4,256]{3,2,1,0:T(4,128)S(1)}, f32[2,18,4,256]{3,2,1,0:T(4,128)S(1)}, u32[]{:S(2)}, u32[]{:S(2)}) collective-permute-start(f32[2,18,4,256]{3,2,1,0:T(4,128)S(1)} %slice.164), channel_id=1, source_target_pairs={{0,1},{1,0},{2,3},{3,2},{4,5},{5,4},{6,7},{7,6},{8,9},{9,8},{10,11... | collective-permute-start | bytes 442376 | tf_op jit(solution)/shard_map/ppermute | solution.py:61
  87.2 6.1 %shard_map.66 = (f32[1,18,4,512]{3,2,1,0:T(4,128)S(1)}, f32[1,18,4,512]{3,2,1,0:T(4,128)S(1)}) custom-call(s32[128]{0:T(128)S(1)} %compare_select_fusion.4.place, bf16[4,672,128]{2,1,0:T(8,128)(2,1)S(1)} %pad_maximum_fusion.1.own, bf16[4,672,128]{2,1,0:T(8,128)(2,1)S(1)} %collective-permute-done.15.other, f32[18,36,8,128]{3,2,1,0:T(8,128)} %copy-done, ...), custom_call_target="tpu_custom_call" | custom-call | flops 4320000000 | bytes 1000000 | tf_op jit(solution)/shard_map/pallas_call | solution.py:200
  93.3 0.9 collective-permute-done.17.left
  94.2 2.5 %collective-permute-start.20 = (f32[18,4,256]{2,1,0:T(4,128)S(1)}, f32[18,4,256]{2,1,0:T(4,128)S(1)}, u32[]{:S(2)}, u32[]{:S(2)}) collective-permute-start(f32[18,4,256]{2,1,0:T(4,128)S(1)} %slice_add_fusion.1), channel_id=1, source_target_pairs={{0,3},{1,2},{2,1},{3,0},{4,7},{5,6},{6,5},{7,4},{8,11},{9,10},{10,... | collective-permute-start | bytes 221192 | tf_op jit(solution)/shard_map/ppermute | solution.py:61
  96.7 1.2 %collective-permute-start.19 = (f32[1,18,4,512]{3,2,1,0:T(4,128)S(1)}, f32[1,18,4,512]{3,2,1,0:T(4,128)S(1)}, u32[]{:S(2)}, u32[]{:S(2)}) collective-permute-start(f32[1,18,4,512]{3,2,1,0:T(4,128)S(1)} %get-tuple-element.24), channel_id=1, source_target_pairs={{0,4},{4,0},{8,12},{12,8},{16,20},{20,16},{24,28},{28,24},{32,36},... | collective-permute-start | bytes 442376 | tf_op jit(solution)/shard_map/ppermute | solution.py:48
  98.1 1.6 %collective-permute-done.20.left_end = f32[18,4,256]{2,1,0:T(4,128)S(1)} collective-permute-done((f32[18,4,256]{2,1,0:T(4,128)S(1)}, f32[18,4,256]{2,1,0:T(4,128)S(1)}, u32[]{:S(2)}, u32[]{:S(2)}) %collective-permute-start.20) | collective-permute-done | bytes 73760 | tf_op jit(solution)/shard_map/ppermute | solution.py:61
  99.7 4.6 %collective-permute-done.21.late_end = f32[18,4,256]{2,1,0:T(4,128)S(1)} collective-permute-done((f32[18,4,256]{2,1,0:T(4,128)S(1)}, f32[18,4,256]{2,1,0:T(4,128)S(1)}, u32[]{:S(2)}, u32[]{:S(2)}) %collective-permute-start.21) | collective-permute-done | bytes 73760 | tf_op jit(solution)/shard_map/ppermute | solution.py:61
  104.2 1.0 shard_map.67
  (59 shorter events, 3.2 us)
Async XLA Ops:
  4.3 1.0 copy-start.2
  4.5 0.8 copy-start.4
  5.3 8.5 %collective-permute-start = (bf16[2,672,128]{2,1,0:T(8,128)(2,1)}, bf16[2,672,128]{2,1,0:T(8,128)(2,1)}, u32[]{:S(2)}, u32[]{:S(2)}) collective-permute-start(bf16[2,672,128]{2,1,0:T(8,128)(2,1)} %fusion.6), channel_id=1, source_target_pairs={{0,4},{4,0},{8,12},{12,8},{16,20},{20,16},{24,28},{28,24},{32,36},... | collective-permute-start | bytes 1032200 | tf_op jit(solution)/shard_map/ppermute | solution.py:48
  9.7 2.2 %copy-start.7 = (s32[2]{0:T(128)S(1)}, s32[2]{0:T(128)}, u32[]{:S(2)}) copy-start(s32[2]{0:T(128)} %param.8) | copy-start | bytes 28
  10.7 4.1 %collective-permute-start.1 = (bf16[2,3,672,128]{3,2,0,1:T(8,128)(2,1)}, bf16[2,3,672,128]{3,2,0,1:T(8,128)(2,1)S(1)}, u32[]{:S(2)}, u32[]{:S(2)}) collective-permute-start(bf16[2,3,672,128]{3,2,0,1:T(8,128)(2,1)} %fusion.2), channel_id=1, source_target_pairs={{0,4},{4,0},{8,12},{12,8},{16,20},{20,16},{24,28},{28,24},{32,36},... | collective-permute-start | bytes 3096584 | tf_op jit(solution)/shard_map/ppermute | solution.py:48
  11.9 1.9 %copy-start.6 = (f32[2,18,2,128]{3,2,1,0:T(2,128)S(1)}, f32[2,18,2,128]{3,2,1,0:T(2,128)}, u32[]{:S(2)}) copy-start(f32[2,18,2,128]{3,2,1,0:T(2,128)} %constant.35.clone) | copy-start | bytes 110596
  15.2 11.4 %collective-permute-start.4 = (bf16[2,672,128]{2,1,0:T(8,128)(2,1)S(1)}, bf16[2,672,128]{2,1,0:T(8,128)(2,1)S(1)}, u32[]{:S(2)}, u32[]{:S(2)}) collective-permute-start(bf16[2,672,128]{2,1,0:T(8,128)(2,1)S(1)} %get-tuple-element.35), channel_id=1, source_target_pairs={{0,192},{4,28},{8,200},{12,20},{16,208},{20,12},{24,216},{28,4},{3... | collective-permute-start | bytes 1032200 | tf_op jit(solution)/shard_map/ppermute | solution.py:48
  16.3 10.3 %collective-permute-start.3 = (bf16[2,672,128]{2,1,0:T(8,128)(2,1)S(1)}, bf16[2,672,128]{2,1,0:T(8,128)(2,1)S(1)}, u32[]{:S(2)}, u32[]{:S(2)}) collective-permute-start(bf16[2,672,128]{2,1,0:T(8,128)(2,1)S(1)} %get-tuple-element.36), channel_id=1, source_target_pairs={{0,128},{4,20},{8,136},{12,28},{16,144},{20,4},{24,152},{28,12},{3... | collective-permute-start | bytes 1032200 | tf_op jit(solution)/shard_map/ppermute | solution.py:48
  16.7 10.6 %collective-permute-start.2 = (bf16[2,672,128]{2,1,0:T(8,128)(2,1)S(1)}, bf16[2,672,128]{2,1,0:T(8,128)(2,1)S(1)}, u32[]{:S(2)}, u32[]{:S(2)}) collective-permute-start(bf16[2,672,128]{2,1,0:T(8,128)(2,1)S(1)} %get-tuple-element.37), channel_id=1, source_target_pairs={{0,64},{4,12},{8,72},{12,4},{16,80},{20,28},{24,88},{28,20},{32,96... | collective-permute-start | bytes 1032200 | tf_op jit(solution)/shard_map/ppermute | solution.py:48
  18.7 8.5 %copy-start.3 = (bf16[1,18,18,2,128]{4,3,2,1,0:T(2,128)(2,1)S(1)}, bf16[1,18,18,2,128]{4,3,2,1,0:T(2,128)(2,1)}, u32[]{:S(2)}) copy-start(bf16[1,18,18,2,128]{4,3,2,1,0:T(2,128)(2,1)} %copy-done.2) | copy-start | bytes 497668
  18.7 8.5 %copy-start.5 = (bf16[1,18,18,2,128]{4,3,2,1,0:T(2,128)(2,1)S(1)}, bf16[1,18,18,2,128]{4,3,2,1,0:T(2,128)(2,1)}, u32[]{:S(2)}) copy-start(bf16[1,18,18,2,128]{4,3,2,1,0:T(2,128)(2,1)} %copy-done.4) | copy-start | bytes 497668
  20.5 27.2 %copy-start = (f32[18,36,8,128]{3,2,1,0:T(8,128)}, f32[18,36,8,128]{3,2,1,0:T(8,128)S(1)}, u32[]{:S(2)}) copy-start(f32[18,36,8,128]{3,2,1,0:T(8,128)S(1)} %shard_map.64.right) | copy-start | bytes 7962628
  28.5 4.6 %collective-permute-start.7 = (bf16[2,168,128]{2,1,0:T(8,128)(2,1)S(1)}, bf16[2,168,128]{2,1,0:T(8,128)(2,1)S(1)}, u32[]{:S(2)}, u32[]{:S(2)}) collective-permute-start(bf16[2,168,128]{2,1,0:T(8,128)(2,1)S(1)} %get-tuple-element.50), channel_id=1, source_target_pairs={{0,24},{4,196},{8,16},{12,204},{16,8},{20,212},{24,0},{28,220},{32... | collective-permute-start | bytes 258056 | tf_op jit(solution)/shard_map/ppermute | solution.py:48
  29.5 4.8 %collective-permute-start.6 = (bf16[2,168,128]{2,1,0:T(8,128)(2,1)S(1)}, bf16[2,168,128]{2,1,0:T(8,128)(2,1)S(1)}, u32[]{:S(2)}, u32[]{:S(2)}) collective-permute-start(bf16[2,168,128]{2,1,0:T(8,128)(2,1)S(1)} %get-tuple-element.51), channel_id=1, source_target_pairs={{0,16},{4,132},{8,24},{12,140},{16,0},{20,148},{24,8},{28,156},{32... | collective-permute-start | bytes 258056 | tf_op jit(solution)/shard_map/ppermute | solution.py:48
  30.0 4.9 %collective-permute-start.5 = (bf16[2,168,128]{2,1,0:T(8,128)(2,1)S(1)}, bf16[2,168,128]{2,1,0:T(8,128)(2,1)S(1)}, u32[]{:S(2)}, u32[]{:S(2)}) collective-permute-start(bf16[2,168,128]{2,1,0:T(8,128)(2,1)S(1)} %get-tuple-element.52), channel_id=1, source_target_pairs={{0,8},{4,68},{8,0},{12,76},{16,24},{20,84},{24,16},{28,92},{32,40}... | collective-permute-start | bytes 258056 | tf_op jit(solution)/shard_map/ppermute | solution.py:48
  34.9 3.4 %collective-permute-start.8 = (bf16[2,168,128]{2,1,0:T(8,128)(2,1)S(1)}, bf16[2,168,128]{2,1,0:T(8,128)(2,1)S(1)}, u32[]{:S(2)}, u32[]{:S(2)}) collective-permute-start(bf16[2,168,128]{2,1,0:T(8,128)(2,1)S(1)} %select_select_fusion.1), channel_id=1, source_target_pairs={{0,32},{4,36},{8,40},{12,44},{16,48},{20,52},{24,56},{28,60},{32,0... | collective-permute-start | bytes 258056 | tf_op jit(solution)/shard_map/ppermute | solution.py:48
  38.4 4.6 %collective-permute-start.11 = (bf16[2,168,128]{2,1,0:T(8,128)(2,1)S(1)}, bf16[2,168,128]{2,1,0:T(8,128)(2,1)S(1)}, u32[]{:S(2)}, u32[]{:S(2)}) collective-permute-start(bf16[2,168,128]{2,1,0:T(8,128)(2,1)S(1)} %broadcast_select_fusion.9), channel_id=1, source_target_pairs={{0,24},{4,196},{8,16},{12,204},{16,8},{20,212},{24,0},{28,220},{32... | collective-permute-start | bytes 258056 | tf_op jit(solution)/shard_map/ppermute | solution.py:48
  39.6 4.8 %collective-permute-start.10 = (bf16[2,168,128]{2,1,0:T(8,128)(2,1)S(1)}, bf16[2,168,128]{2,1,0:T(8,128)(2,1)S(1)}, u32[]{:S(2)}, u32[]{:S(2)}) collective-permute-start(bf16[2,168,128]{2,1,0:T(8,128)(2,1)S(1)} %broadcast_select_fusion.9), channel_id=1, source_target_pairs={{0,16},{4,132},{8,24},{12,140},{16,0},{20,148},{24,8},{28,156},{32... | collective-permute-start | bytes 258056 | tf_op jit(solution)/shard_map/ppermute | solution.py:48
  40.5 4.0 %collective-permute-start.9 = (bf16[2,168,128]{2,1,0:T(8,128)(2,1)S(1)}, bf16[2,168,128]{2,1,0:T(8,128)(2,1)S(1)}, u32[]{:S(2)}, u32[]{:S(2)}) collective-permute-start(bf16[2,168,128]{2,1,0:T(8,128)(2,1)S(1)} %broadcast_select_fusion.9), channel_id=1, source_target_pairs={{0,8},{4,68},{8,0},{12,76},{16,24},{20,84},{24,16},{28,92},{32,40}... | collective-permute-start | bytes 258056 | tf_op jit(solution)/shard_map/ppermute | solution.py:48
  44.5 9.6 %collective-permute-start.13 = (bf16[2,672,128]{2,1,0:T(8,128)(2,1)S(1)}, bf16[2,672,128]{2,1,0:T(8,128)(2,1)S(1)}, u32[]{:S(2)}, u32[]{:S(2)}) collective-permute-start(bf16[2,672,128]{2,1,0:T(8,128)(2,1)S(1)} %pad_maximum_fusion.3), channel_id=1, source_target_pairs={{0,128},{4,20},{8,136},{12,28},{16,144},{20,4},{24,152},{28,12},{3... | collective-permute-start | bytes 1032200 | tf_op jit(solution)/shard_map/ppermute | solution.py:48
  47.2 9.8 %collective-permute-start.12 = (bf16[2,672,128]{2,1,0:T(8,128)(2,1)S(1)}, bf16[2,672,128]{2,1,0:T(8,128)(2,1)S(1)}, u32[]{:S(2)}, u32[]{:S(2)}) collective-permute-start(bf16[2,672,128]{2,1,0:T(8,128)(2,1)S(1)} %pad_maximum_fusion.3), channel_id=1, source_target_pairs={{0,64},{4,12},{8,72},{12,4},{16,80},{20,28},{24,88},{28,20},{32,96... | collective-permute-start | bytes 1032200 | tf_op jit(solution)/shard_map/ppermute | solution.py:48
  47.7 9.9 %collective-permute-start.14 = (bf16[2,672,128]{2,1,0:T(8,128)(2,1)S(1)}, bf16[2,672,128]{2,1,0:T(8,128)(2,1)S(1)}, u32[]{:S(2)}, u32[]{:S(2)}) collective-permute-start(bf16[2,672,128]{2,1,0:T(8,128)(2,1)S(1)} %pad_maximum_fusion.3), channel_id=1, source_target_pairs={{0,192},{4,28},{8,200},{12,20},{16,208},{20,12},{24,216},{28,4},{3... | collective-permute-start | bytes 1032200 | tf_op jit(solution)/shard_map/ppermute | solution.py:48
  57.8 8.1 %collective-permute-start.15 = (bf16[4,672,128]{2,1,0:T(8,128)(2,1)S(1)}, bf16[4,672,128]{2,1,0:T(8,128)(2,1)S(1)}, u32[]{:S(2)}, u32[]{:S(2)}) collective-permute-start(bf16[4,672,128]{2,1,0:T(8,128)(2,1)S(1)} %pad_maximum_fusion.2), channel_id=1, source_target_pairs={{0,4},{4,0},{8,12},{12,8},{16,20},{20,16},{24,28},{28,24},{32,36},... | collective-permute-start | bytes 2064392 | tf_op jit(solution)/shard_map/ppermute | solution.py:48
  77.6 1.9 %collective-permute-start.16 = (f32[3,18,4,512]{3,2,1,0:T(4,128)S(1)}, f32[3,18,4,512]{3,2,1,0:T(4,128)S(1)}, u32[]{:S(2)}, u32[]{:S(2)}) collective-permute-start(f32[3,18,4,512]{3,2,1,0:T(4,128)S(1)} %get-tuple-element.19), channel_id=1, source_target_pairs={{0,4},{4,0},{8,12},{12,8},{16,20},{20,16},{24,28},{28,24},{32,36},... | collective-permute-start | bytes 1327112 | tf_op jit(solution)/shard_map/ppermute | solution.py:48
  79.7 24.5 %copy-start.1 = (f32[256,256]{1,0:T(8,128)S(1)}, f32[256,256]{1,0:T(8,128)}, u32[]{:S(2)}) copy-start(f32[256,256]{1,0:T(8,128)} %constant.37.clone.flip) | copy-start | bytes 786436
  79.7 13.5 %collective-permute-start.18 = (f32[2,18,4,256]{3,2,1,0:T(4,128)S(1)}, f32[2,18,4,256]{3,2,1,0:T(4,128)S(1)}, u32[]{:S(2)}, u32[]{:S(2)}) collective-permute-start(f32[2,18,4,256]{3,2,1,0:T(4,128)S(1)} %pad_maximum_fusion.4), channel_id=1, source_target_pairs={{0,3},{1,2},{2,1},{3,0},{4,7},{5,6},{6,5},{7,4},{8,11},{9,10},{10,... | collective-permute-start | bytes 442376 | tf_op jit(solution)/shard_map/ppermute | solution.py:61
  86.0 8.2 %collective-permute-start.17 = (f32[2,18,4,256]{3,2,1,0:T(4,128)S(1)}, f32[2,18,4,256]{3,2,1,0:T(4,128)S(1)}, u32[]{:S(2)}, u32[]{:S(2)}) collective-permute-start(f32[2,18,4,256]{3,2,1,0:T(4,128)S(1)} %slice.164), channel_id=1, source_target_pairs={{0,1},{1,0},{2,3},{3,2},{4,5},{5,4},{6,7},{7,6},{8,9},{9,8},{10,11... | collective-permute-start | bytes 442376 | tf_op jit(solution)/shard_map/ppermute | solution.py:61
  94.2 5.5 %collective-permute-start.20 = (f32[18,4,256]{2,1,0:T(4,128)S(1)}, f32[18,4,256]{2,1,0:T(4,128)S(1)}, u32[]{:S(2)}, u32[]{:S(2)}) collective-permute-start(f32[18,4,256]{2,1,0:T(4,128)S(1)} %slice_add_fusion.1), channel_id=1, source_target_pairs={{0,3},{1,2},{2,1},{3,0},{4,7},{5,6},{6,5},{7,4},{8,11},{9,10},{10,... | collective-permute-start | bytes 221192 | tf_op jit(solution)/shard_map/ppermute | solution.py:61
  96.7 7.5 %collective-permute-start.19 = (f32[1,18,4,512]{3,2,1,0:T(4,128)S(1)}, f32[1,18,4,512]{3,2,1,0:T(4,128)S(1)}, u32[]{:S(2)}, u32[]{:S(2)}) collective-permute-start(f32[1,18,4,512]{3,2,1,0:T(4,128)S(1)} %get-tuple-element.24), channel_id=1, source_target_pairs={{0,4},{4,0},{8,12},{12,8},{16,20},{20,16},{24,28},{28,24},{32,36},... | collective-permute-start | bytes 442376 | tf_op jit(solution)/shard_map/ppermute | solution.py:48
  98.0 6.3 %collective-permute-start.21 = (f32[18,4,256]{2,1,0:T(4,128)S(1)}, f32[18,4,256]{2,1,0:T(4,128)S(1)}, u32[]{:S(2)}, u32[]{:S(2)}) collective-permute-start(f32[18,4,256]{2,1,0:T(4,128)S(1)} %slice_add_fusion), channel_id=1, source_target_pairs={{0,1},{1,0},{2,3},{3,2},{4,5},{5,4},{6,7},{7,6},{8,9},{9,8},{10,11... | collective-permute-start | bytes 221192 | tf_op jit(solution)/shard_map/ppermute | solution.py:61
